TPU v7x, 256 devices: a whole 4x4x8 slice. The times are simulated.
256 devices in a mesh: group: 2 (over z_hi), seq: 16 (over z_lo, x), mp: 8 (over y, core).
Axes of the slice: x: 4, y: 4, z: 8 (z_hi: 2, z_lo: 4; z = z_hi * 4 + z_lo), core: 2. Of those that a mesh axis runs over, the one named last changes fastest.
Arguments:
- image_states: bfloat16 [16, 256, 7680], P('seq'), may hold values from -6 to 6
- norm_gain: float32 [1280], replicated, may hold values from 0.1 to 1.9
- proj_weight: bfloat16 [7680, 8192], P('seq', 'mp'), may hold values from -0.0625 to 0.0625
- kv_weight: bfloat16 [8192, 2048], P('mp'), may hold values from -0.0625 to 0.0625
- key_gain: float32 [128], replicated, may hold values from 0.1 to 1.9
- queries: bfloat16 [4096, 8192], P('seq', 'mp'), may hold values from -6 to 6
- query_gain: float32 [128], replicated, may hold values from 0.1 to 1.9
- head_gate: float32 [64], P('mp'), may hold values from 0.3 to 1.5
- cotangent: bfloat16 [4096, 8192], P('seq', 'mp'), may hold values from -192 to 192
- block_image: int32 [256, 1], P('seq'), may hold values from 0 to 15; in each aligned block of 16 rows (0 to 15, 16 to 31, ...) at most 2 rows name the same one
- image_len: int32 [16], replicated, may hold values from 64 to 256, as said below
Outputs:
- gradients: bfloat16 [2, 4096, 8192], P('group', 'seq', 'mp')
Inputs may be any that keep to these rules, and one draw needn't show every extreme that they name: Text tokens b * 16 to (b + 1) * 16 - 1 attend the image block_image[b, 0]; within the 16 text blocks of one index of seq (aligned blocks of rows) no image is attended by more than 2 text blocks. Image i holds image_len[i] tokens; its key slots from image_len[i] on are left out.
All inputs are finite; a program needn't handle non-finite values.
Results may differ from a plain program's by a relative error of at most 0.013.
Values may be sent and summed in bfloat16 or wider, within the bound.
A program may use at most 128 MiB of HBM per device.

v0:
```python
import math

import jax
import jax.numpy as jnp
from jax import lax
from jax.sharding import PartitionSpec as P

epsilon = 1e-05


def passed_along(x, axis, by):
    length = lax.axis_size(axis)
    pairs = [(i, i + by) for i in range(length) if 0 <= i + by < length]
    return lax.ppermute(x, axis, pairs)


def root_scaled(values, scales):
    return values * lax.rsqrt(jnp.mean(values * values, axis=-1, keepdims=True) + epsilon) * scales


def per_device(
    image_states,
    norm_gain,
    proj_weight,
    kv_weight,
    key_gain,
    queries,
    query_gain,
    head_gate,
    cotangent,
    block_image,
    image_len,
):
    vision = lax.axis_index("group") == 0
    images_here, image_rows, input_width = image_states.shape
    norm_width = norm_gain.shape[0]
    own_rows = images_here * image_rows
    head_size = key_gain.shape[0]
    kv_width = kv_weight.shape[1] // lax.axis_size("mp")
    kv_here = kv_width // (2 * head_size)
    feature_cols = proj_weight.shape[1]
    image_count = image_len.shape[0]
    flattened = image_states.reshape(own_rows, input_width)
    leading = flattened[:, :norm_width].astype(jnp.float32)
    center = jnp.mean(leading, axis=-1, keepdims=True)
    spread = jnp.mean((leading - center) ** 2, axis=-1, keepdims=True)
    normed_lead = ((leading - center) * lax.rsqrt(spread + epsilon) * norm_gain).astype(
        jnp.bfloat16
    )
    normed = jnp.concatenate([normed_lead, flattened[:, norm_width:]], axis=1)
    portion = lax.all_gather(proj_weight, "seq", axis=0, tiled=True)

    def accumulate(carried):
        return jnp.dot(normed, portion, preferred_element_type=jnp.float32)

    def unchanged(carried):
        return carried

    features = lax.cond(
        vision, accumulate, unchanged, jnp.zeros((own_rows, feature_cols), jnp.float32)
    ).astype(jnp.bfloat16)

    def project(feature_rows):
        return jnp.dot(feature_rows, kv_weight, preferred_element_type=jnp.float32)

    def skipped_project(feature_rows):
        return jnp.zeros((own_rows, kv_weight.shape[1]), jnp.float32)

    pieces = lax.cond(vision, project, skipped_project, features)
    projected = lax.psum_scatter(pieces, "mp", scatter_dimension=1, tiled=True).reshape(
        own_rows, kv_here, 2, head_size
    )

    def key_normed(incoming):
        return root_scaled(incoming, key_gain)

    def query_normed(incoming):
        return root_scaled(incoming, query_gain)

    keys_out, key_back = jax.vjp(key_normed, projected[:, :, 0])
    keyval = jnp.stack(
        [keys_out.astype(jnp.bfloat16), projected[:, :, 1].astype(jnp.bfloat16)], axis=2
    ).reshape(images_here, image_rows, kv_width)
    tokens_here, column_count = queries.shape
    blocks = block_image.shape[0]
    block_rows = tokens_here // blocks
    heads_here = head_gate.shape[0]
    group_size = heads_here // kv_here
    inverse_root = 1.0 / math.sqrt(head_size)
    chosen_image = block_image[:, 0]
    query_blocks = queries.reshape(blocks, block_rows, column_count)
    cot_blocks = cotangent.reshape(blocks, block_rows, column_count)

    def lengths_of(image_ids):
        return jnp.sum(
            jnp.where(
                image_ids[:, None] == jnp.arange(image_count, dtype=jnp.int32)[None, :],
                image_len[None, :],
                0,
            ),
            axis=1,
        )

    def attend_core(query_rows, cot_rows, chosen, lengths):
        block_count = query_rows.shape[0]
        query_wide = query_rows.astype(jnp.float32).reshape(
            block_count * block_rows, heads_here, head_size
        )
        query_out, query_back = jax.vjp(query_normed, query_wide)
        query_low = query_out.astype(jnp.bfloat16).reshape(
            block_count, block_rows, kv_here, group_size, head_size
        )
        chosen = chosen.reshape(block_count, image_rows, kv_here, 2, head_size)
        chosen_keys = chosen[:, :, :, 0]
        chosen_values = chosen[:, :, :, 1]
        usable = (jnp.arange(image_rows, dtype=jnp.int32)[None, :] < lengths[:, None]).astype(
            jnp.float32
        )
        scores = (
            jnp.einsum(
                "btkgd,bjkd->bkgtj", query_low, chosen_keys, preferred_element_type=jnp.float32
            )
            * inverse_root
        )
        raised = jnp.exp(scores) * usable[:, None, None, None, :]
        weights = raised / jnp.sum(raised, axis=-1, keepdims=True)
        weights_low = weights.astype(jnp.bfloat16)
        gate_values = jnp.tanh(head_gate).reshape(kv_here, group_size)
        grad_low = (
            cot_rows.astype(jnp.float32).reshape(
                block_count, block_rows, kv_here, group_size, head_size
            )
            * gate_values[None, None, :, :, None]
        ).astype(jnp.bfloat16)
        weight_grads = jnp.einsum(
            "btkgd,bjkd->bkgtj", grad_low, chosen_values, preferred_element_type=jnp.float32
        )
        row_inner = jnp.sum(weights * weight_grads, axis=-1, keepdims=True)
        score_grads = (weights * (weight_grads - row_inner) * inverse_root).astype(jnp.bfloat16)
        query_grads = jnp.einsum(
            "bkgtj,bjkd->btkgd", score_grads, chosen_keys, preferred_element_type=jnp.float32
        ).reshape(block_count * block_rows, heads_here, head_size)
        query_result = (
            query_back(query_grads)[0]
            .reshape(block_count * block_rows, heads_here * head_size)
            .astype(jnp.bfloat16)
        )
        key_grads = jnp.einsum(
            "bkgtj,btkgd->bjkd", score_grads, query_low, preferred_element_type=jnp.float32
        )
        value_grads = jnp.einsum(
            "bkgtj,btkgd->bjkd", weights_low, grad_low, preferred_element_type=jnp.float32
        )
        block_grads = jnp.stack([key_grads, value_grads], axis=3).reshape(
            block_count, image_rows * kv_width
        )
        return (query_result, block_grads)

    gathered = lax.all_gather(keyval, "seq", axis=0, tiled=True)
    every_image = passed_along(gathered, "group", 1)

    def attend_all(images_all):
        chosen = jnp.take(images_all, chosen_image, axis=0)
        return attend_core(query_blocks, cot_blocks, chosen, lengths_of(chosen_image))

    def skipped_all(images_all):
        return (
            jnp.zeros((tokens_here, column_count), jnp.bfloat16),
            jnp.zeros((blocks, image_rows * kv_width), jnp.float32),
        )

    query_result, block_grads = lax.cond(vision, skipped_all, attend_all, every_image)
    image_ids = jnp.arange(lax.axis_size("seq") * own_rows // image_rows, dtype=jnp.int32)
    membership = (image_ids[:, None] == chosen_image[None, :]).astype(jnp.float32)
    summed = jnp.dot(
        membership, block_grads, precision=lax.Precision.HIGHEST, preferred_element_type=jnp.float32
    )
    own_sum = lax.psum_scatter(
        summed.reshape(lax.axis_size("seq") * own_rows, kv_width),
        "seq",
        scatter_dimension=0,
        tiled=True,
    )
    returned = passed_along(own_sum, "group", -1)
    returned = returned.reshape(own_rows, kv_here, 2, head_size)
    key_raw_grads = key_back(returned[:, :, 0])[0]
    projected_grads = (
        jnp.stack([key_raw_grads, returned[:, :, 1]], axis=2)
        .reshape(own_rows, kv_width)
        .astype(jnp.bfloat16)
    )
    add_portion = lax.all_gather(projected_grads, "mp", axis=1, tiled=True)

    def accumulate(carried):
        return lax.dot_general(
            add_portion, kv_weight, (((1,), (1,)), ((), ())), preferred_element_type=jnp.float32
        )

    def unchanged(carried):
        return carried

    feature_grads = lax.cond(
        vision, accumulate, unchanged, jnp.zeros((own_rows, feature_cols), jnp.float32)
    ).astype(jnp.bfloat16)
    result = jnp.where(vision, feature_grads, query_result)
    return result[None]


def solution(mesh):
    placed = (
        P("seq", None, None),
        P(),
        P("seq", "mp"),
        P("mp", None),
        P(),
        P("seq", "mp"),
        P(),
        P("mp"),
        P("seq", "mp"),
        P("seq", None),
        P(),
    )
    return jax.shard_map(
        per_device, mesh=mesh, in_specs=placed, out_specs=P("group", "seq", "mp"), check_vma=False
    )
```

profile of v0, /device:TPU:1, one launch (start us, length us, event | category | flops | bytes accessed | tf_op | source)
XLA Modules:
  0.0 597.7 jit_solution(18182204975133798700)
XLA Ops:
  6.5 0.7 all-gather.4.cloned.1.call-update
  7.3 2.1 slice.37
  9.5 1.3 convert_reduce_fusion
  10.7 1.4 fusion.22
  12.2 1.4 fusion.24
  13.5 2.2 pad_maximum_fusion.1
  15.7 173.5 %all-gather.4.cloned.1.call-done = bf16[7680,1024]{1,0:T(8,128)(2,1)} async-done(((bf16[480,1024]{1,0:T(8,128)(2,1)}), bf16[7680,1024]{1,0:T(8,128)(2,1)}) %all-gather.4.cloned.1.call-update) | async-done | bytes 15728656 | tf_op jit(solution)/shard_map/all_gather | solution.py:51
  189.1 10.9 %conditional.4 = (bf16[256,1024]{1,0:T(8,128)(2,1)S(1)}) conditional(s32[]{:T(128)} %convert_element_type.91, () %tuple.37, (bf16[256,7680]{1,0:T(8,128)(2,1)}, bf16[7680,1024]{1,0:T(8,128)(2,1)}) %tuple.38), branch_computations={%region_2.0_spmd, %region_3.0_spmd} | conditional | flops 4026793984 | bytes 20185096 | solution.py:59
  189.1 10.9 %convolution_convert_fusion = bf16[256,1024]{1,0:T(8,128)(2,1)S(1)} fusion(bf16[256,7680]{1,0:T(8,128)(2,1)} %get-tuple-element.46, bf16[7680,1024]{1,0:T(8,128)(2,1)} %get-tuple-element.47), kind=kOutput, calls=%fused_computation.1 | convolution fusion | flops 4026793984 | bytes 20185088 | tf_op jit(solution)/shard_map/cond/branch_1_fun/dot_general | solution.py:54
  200.0 3.5 conditional.5
  200.1 3.4 fusion.32
  203.5 1.9 copy.95
  205.5 28.3 %reduce-scatter.3.cloned.1.call-done = f32[256,256]{0,1:T(8,128)} async-done(((f32[256,2048]{0,1:T(8,128)}), f32[256,256]{0,1:T(8,128)}) %reduce-scatter.3.cloned.1.call-update) | async-done | bytes 262160 | tf_op jit(solution)/shard_map/reduce_scatter | solution.py:70
  233.8 0.9 slice.38
  234.7 0.9 slice.39
  236.2 0.8 copy.99
  237.0 75.2 %all-gather.6.cloned.1.call-done = bf16[16,256,256]{2,1,0:T(8,128)(2,1)} async-done(((bf16[1,256,256]{2,1,0:T(8,128)(2,1)}), bf16[16,256,256]{2,1,0:T(8,128)(2,1)}) %all-gather.6.cloned.1.call-update) | async-done | bytes 2097168 | tf_op jit(solution)/shard_map/all_gather | solution.py:159
  312.3 6.3 %collective-permute-start = (bf16[16,256,256]{2,1,0:T(8,128)(2,1)}, bf16[16,256,256]{2,1,0:T(8,128)(2,1)S(1)}, u32[]{:S(2)}, u32[]{:S(2)}) collective-permute-start(bf16[16,256,256]{2,1,0:T(8,128)(2,1)} %all-gather.6.cloned.1.call-done), channel_id=1, source_target_pairs={{0,128},{1,129},{2,130},{3,131},{4,132},{5,133},{6,134},{7,135},{8... | collective-permute-start | bytes 6291464 | tf_op jit(solution)/shard_map/ppermute | solution.py:14
  318.5 34.4 %collective-permute-done = bf16[16,256,256]{2,1,0:T(8,128)(2,1)S(1)} collective-permute-done((bf16[16,256,256]{2,1,0:T(8,128)(2,1)}, bf16[16,256,256]{2,1,0:T(8,128)(2,1)S(1)}, u32[]{:S(2)}, u32[]{:S(2)}) %collective-permute-start) | collective-permute-done | bytes 2097184 | tf_op jit(solution)/shard_map/ppermute | solution.py:14
  352.9 2.7 conditional.6
  353.1 2.3 broadcast.204
  355.7 6.2 %fusion.29 = f32[16,65536]{1,0:T(8,128)} fusion(f32[16,65536]{1,0:T(8,128)} %get-tuple-element.62, s32[16]{0:T(128)S(1)} %bitcast.166), kind=kOutput, calls=%fused_computation.71 | convolution fusion | flops 201326848 | bytes 8388672 | tf_op jit(solution)/shard_map/dot_general | solution.py:175
  361.9 3.9 reshape.292
  365.8 5.7 copy.100
  371.5 170.3 %reduce-scatter.5.cloned.1.call-done = f32[256,256]{0,1:T(8,128)} async-done(((f32[4096,256]{0,1:T(8,128)}), f32[256,256]{0,1:T(8,128)}) %reduce-scatter.5.cloned.1.call-update) | async-done | bytes 262160 | tf_op jit(solution)/shard_map/reduce_scatter | solution.py:178
  541.8 1.3 collective-permute-start.1
  543.1 10.0 %collective-permute-done.1 = f32[256,256]{0,1:T(8,128)S(1)} collective-permute-done((f32[256,256]{0,1:T(8,128)}, f32[256,256]{0,1:T(8,128)S(1)}, u32[]{:S(2)}, u32[]{:S(2)}) %collective-permute-start.1) | collective-permute-done | bytes 262176 | tf_op jit(solution)/shard_map/ppermute | solution.py:14
  553.7 0.8 copy.103
  554.5 32.0 %all-gather.8.cloned.1.call-done = bf16[256,2048]{0,1:T(8,128)(2,1)} async-done(((bf16[256,256]{0,1:T(8,128)(2,1)}), bf16[256,2048]{0,1:T(8,128)(2,1)}) %all-gather.8.cloned.1.call-update) | async-done | bytes 1048592 | tf_op jit(solution)/shard_map/all_gather | solution.py:192
  586.5 3.8 conditional.7
  586.5 3.8 convolution_convert_fusion.1
  590.3 0.9 select_bitcast_fusion
  (43 shorter events, 1.4 us)
Async XLA Ops:
  6.5 182.6 %all-gather.4.cloned.1.call-start = ((), (), s32[]{:S(2)}) async-start(), calls=%async_computation.2 | async-start | bytes 16711680 | tf_op jit(solution)/shard_map/all_gather | solution.py:51
  7.3 226.5 %reduce-scatter.3.cloned.1.call-start = ((), (), s32[]{:S(2)}) async-start(), calls=%async_computation.3 | async-start | bytes 2359296 | tf_op jit(solution)/shard_map/reduce_scatter | solution.py:70
  7.3 4.8 copy-start.7
  205.4 30.6 %copy-start.8 = (f32[128]{0:T(128)S(1)}, f32[128]{0:T(128)}, u32[]{:S(2)}) copy-start(f32[128]{0:T(128)} %param.23) | copy-start | bytes 1540
  205.4 147.5 %copy-start.3 = (bf16[256,1024]{1,0:T(8,128)(2,1)S(1)}, bf16[256,1024]{1,0:T(8,128)(2,1)}, u32[]{:S(2)}) copy-start(bf16[256,1024]{1,0:T(8,128)(2,1)} %param.24) | copy-start | bytes 1572868
  205.4 147.5 %copy-start.6 = (bf16[256,1024]{1,0:T(8,128)(2,1)S(1)}, bf16[256,1024]{1,0:T(8,128)(2,1)}, u32[]{:S(2)}) copy-start(bf16[256,1024]{1,0:T(8,128)(2,1)} %param.27) | copy-start | bytes 1572868
  205.4 147.5 %copy-start.9 = (f32[128]{0:T(128)S(1)}, f32[128]{0:T(128)}, u32[]{:S(2)}) copy-start(f32[128]{0:T(128)} %param.25) | copy-start | bytes 1540
  205.4 147.5 %copy-start.10 = (s32[16,1]{0,1:T(1,128)S(1)}, s32[16,1]{0,1:T(1,128)}, u32[]{:S(2)}) copy-start(s32[16,1]{0,1:T(1,128)} %param.28) | copy-start | bytes 196
  205.4 147.5 %copy-start.11 = (s32[16]{0:T(128)S(1)}, s32[16]{0:T(128)}, u32[]{:S(2)}) copy-start(s32[16]{0:T(128)} %param.29) | copy-start | bytes 196
  205.4 147.5 %copy-start.12 = (f32[8]{0:T(128)S(1)}, f32[8]{0:T(128)}, u32[]{:S(2)}) copy-start(f32[8]{0:T(128)} %param.26) | copy-start | bytes 100
  205.4 106.8 %all-gather.6.cloned.1.call-start = ((), (), s32[]{:S(2)}) async-start(), calls=%async_computation.4 | async-start | bytes 2228224 | tf_op jit(solution)/shard_map/all_gather | solution.py:159
  237.0 304.8 %reduce-scatter.5.cloned.1.call-start = ((), (), s32[]{:S(2)}) async-start(), calls=%async_computation.5 | async-start | bytes 4456448 | tf_op jit(solution)/shard_map/reduce_scatter | solution.py:178
  312.3 40.6 %collective-permute-start = (bf16[16,256,256]{2,1,0:T(8,128)(2,1)}, bf16[16,256,256]{2,1,0:T(8,128)(2,1)S(1)}, u32[]{:S(2)}, u32[]{:S(2)}) collective-permute-start(bf16[16,256,256]{2,1,0:T(8,128)(2,1)} %all-gather.6.cloned.1.call-done), channel_id=1, source_target_pairs={{0,128},{1,129},{2,130},{3,131},{4,132},{5,133},{6,134},{7,135},{8... | collective-permute-start | bytes 6291464 | tf_op jit(solution)/shard_map/ppermute | solution.py:14
  371.4 215.1 %all-gather.8.cloned.1.call-start = ((), (), s32[]{:S(2)}) async-start(), calls=%async_computation.6 | async-start | bytes 1179648 | tf_op jit(solution)/shard_map/all_gather | solution.py:192
  541.8 11.3 %collective-permute-start.1 = (f32[256,256]{0,1:T(8,128)}, f32[256,256]{0,1:T(8,128)S(1)}, u32[]{:S(2)}, u32[]{:S(2)}) collective-permute-start(f32[256,256]{0,1:T(8,128)} %reduce-scatter.5.cloned.1.call-done), channel_id=1, source_target_pairs={{128,0},{129,1},{130,2},{131,3},{132,4},{133,5},{134,6},{135,7},{1... | collective-permute-start | bytes 786440 | tf_op jit(solution)/shard_map/ppermute | solution.py:14
Sparse Core Ops, SparseCore 0:
  9.1 179.9 all-gather.3
  205.6 28.1 reduce-scatter.2
  237.1 75.1 all-gather.5
  371.6 170.1 reduce-scatter.4
  554.6 31.8 all-gather.7
where the time goes:
time: 598 us
  waiting for transfers between devices  524 us (88%)
  matrix products  24.3 us (4%)
  local copies, waits for them, and re-layouts  19.8 us (3%)
  between operations  13.4 us (2%)
  starting transfers between devices  7.7 us (1%)
  other arithmetic  7.57 us (1%)
    all_gather x1, waiting for transfers between devices, per_device(): portion = lax.all_gather(proj_weight, 'seq', axis=0, tiled=True)  173 us
    reduce_scatter x1, waiting for transfers between devices, per_device(): lax.psum_scatter(summed.reshape(lax.axis_size('seq') * own_rows, kv_width...  170 us
    all_gather x1, waiting for transfers between devices, per_device(): gathered = lax.all_gather(keyval, 'seq', axis=0, tiled=True)  75.2 us
    ppermute x2, waiting for transfers between devices, passed_along(): return lax.ppermute(x, axis, pairs)  44.4 us
    all_gather x1, waiting for transfers between devices, per_device(): add_portion = lax.all_gather(projected_grads, 'mp', axis=1, tiled=True)  32 us
    reduce_scatter x1, waiting for transfers between devices, per_device(): lax.psum_scatter(pieces, 'mp', scatter_dimension=1, tiled=True)  28.3 us
  transfers between devices with their start and end apart: 7, of which 7 were waited for; matrix products, arithmetic and copies ran while one was open for 1% of the time, Pallas kernels for 0%

commit v1 on v0

--- a/solution.py
+++ b/solution.py
@@ -48,26 +48,12 @@
         jnp.bfloat16
     )
     normed = jnp.concatenate([normed_lead, flattened[:, norm_width:]], axis=1)
-    portion = lax.all_gather(proj_weight, "seq", axis=0, tiled=True)
-
-    def accumulate(carried):
-        return jnp.dot(normed, portion, preferred_element_type=jnp.float32)
-
-    def unchanged(carried):
-        return carried
-
-    features = lax.cond(
-        vision, accumulate, unchanged, jnp.zeros((own_rows, feature_cols), jnp.float32)
-    ).astype(jnp.bfloat16)
-
-    def project(feature_rows):
-        return jnp.dot(feature_rows, kv_weight, preferred_element_type=jnp.float32)
-
-    def skipped_project(feature_rows):
-        return jnp.zeros((own_rows, kv_weight.shape[1]), jnp.float32)
-
-    pieces = lax.cond(vision, project, skipped_project, features)
-    projected = lax.psum_scatter(pieces, "mp", scatter_dimension=1, tiled=True).reshape(
+    portion = jnp.dot(proj_weight, kv_weight, preferred_element_type=jnp.float32)
+    portion = lax.psum_scatter(
+        portion.astype(jnp.bfloat16), "mp", scatter_dimension=1, tiled=True
+    )
+    portion = lax.all_gather(portion, "seq", axis=0, tiled=True)
+    projected = jnp.dot(normed, portion, preferred_element_type=jnp.float32).reshape(
         own_rows, kv_here, 2, head_size
     )
 
@@ -157,7 +143,7 @@
         return (query_result, block_grads)
 
     gathered = lax.all_gather(keyval, "seq", axis=0, tiled=True)
-    every_image = passed_along(gathered, "group", 1)
+    every_image = gathered
 
     def attend_all(images_all):
         chosen = jnp.take(images_all, chosen_image, axis=0)
@@ -176,13 +162,13 @@
         membership, block_grads, precision=lax.Precision.HIGHEST, preferred_element_type=jnp.float32
     )
     own_sum = lax.psum_scatter(
-        summed.reshape(lax.axis_size("seq") * own_rows, kv_width),
+        summed.reshape(lax.axis_size("seq") * own_rows, kv_width).astype(jnp.bfloat16),
         "seq",
         scatter_dimension=0,
         tiled=True,
     )
     returned = passed_along(own_sum, "group", -1)
-    returned = returned.reshape(own_rows, kv_here, 2, head_size)
+    returned = returned.astype(jnp.float32).reshape(own_rows, kv_here, 2, head_size)
     key_raw_grads = key_back(returned[:, :, 0])[0]
     projected_grads = (
         jnp.stack([key_raw_grads, returned[:, :, 1]], axis=2)

time: 598 us -> 412 us (0.69)
  waiting for transfers between devices: 524 us -> 363 us
  local copies, waits for them, and re-layouts: 19.8 us -> 11.7 us
  starting transfers between devices: 7.7 us -> 1.44 us
    all_gather x1, waiting for transfers between devices: 173 us -> 76.9 us  [per_device(): portion = lax.all_gather(portion, 'seq', axis=0, tiled=True)]
    reduce_scatter x1, waiting for transfers between devices: 170 us -> 126 us  [per_device(): lax.psum_scatter(summed.reshape(lax.axis_size('seq') * own_rows, kv_width...]
    ppermute x2 -> x1, waiting for transfers between devices: 44.4 us -> 9.06 us  [passed_along(): return lax.ppermute(x, axis, pairs)]
    reshape x2 -> x0, local copies, waits for them, and re-layouts: 9.54 us -> none  [per_device(): summed.reshape(lax.axis_size('seq') * own_rows, kv_width)]
    reduce_scatter x1, waiting for transfers between devices: 28.3 us -> 37.2 us  [per_device(): lax.psum_scatter(portion.astype(jnp.bfloat16), 'mp', scatter_dimension=1,...]
    ppermute x2 -> x1, starting transfers between devices: 7.54 us -> 1.28 us  [passed_along(): return lax.ppermute(x, axis, pairs)]
  transfers between devices with their start and end apart: 7 -> 6, of which waited for: 7 -> 6; matrix products, arithmetic and copies ran while one was open for 1% -> 1% of each run, Pallas kernels for 0% -> 0%
where the time goes in v1:
time: 412 us; the launch traced here: 411 us
  waiting for transfers between devices  363 us (88%)
  matrix products  18.8 us (5%)
  between operations  13.4 us (3%)
  local copies, waits for them, and re-layouts  11.7 us (3%)
    reduce_scatter x1, waiting for transfers between devices, per_device(): lax.psum_scatter(summed.reshape(lax.axis_size('seq') * own_rows, kv_width...  126 us
    all_gather x1, waiting for transfers between devices, per_device(): gathered = lax.all_gather(keyval, 'seq', axis=0, tiled=True)  81.2 us
    all_gather x1, waiting for transfers between devices, per_device(): portion = lax.all_gather(portion, 'seq', axis=0, tiled=True)  76.9 us
    reduce_scatter x1, waiting for transfers between devices, per_device(): lax.psum_scatter(portion.astype(jnp.bfloat16), 'mp', scatter_dimension=1,...  37.2 us
    all_gather x1, waiting for transfers between devices, per_device(): add_portion = lax.all_gather(projected_grads, 'mp', axis=1, tiled=True)  32.6 us
    ppermute x1, waiting for transfers between devices, passed_along(): return lax.ppermute(x, axis, pairs)  9.06 us
  transfers between devices with their start and end apart: 6, of which 6 were waited for; matrix products, arithmetic and copies ran while one was open for 1% of the time, Pallas kernels for 0%

profile of v1, /device:TPU:1, one launch (start us, length us, event | category | flops | bytes accessed | tf_op | source)
XLA Modules:
  0.0 411.0 jit_solution(5862694698732804078)
XLA Ops:
  6.5 1.2 copy-done
  7.7 5.7 %convolution_convert_fusion.2 = bf16[480,2048]{1,0:T(8,128)(2,1)} fusion(bf16[480,1024]{1,0:T(8,128)(2,1)S(1)} %copy-done, bf16[1024,2048]{1,0:T(8,128)(2,1)} %param.18), kind=kOutput, calls=%fused_computation.55 | convolution fusion | flops 2014248960 | bytes 7143424 | tf_op jit(solution)/shard_map/dot_general | solution.py:51
  13.5 0.0 all-gather.4.cloned.1.call-start
  13.5 37.2 %reduce-scatter.3.cloned.1.call-done = bf16[480,256]{1,0:T(8,128)(2,1)} async-done(((bf16[480,2048]{1,0:T(8,128)(2,1)}), bf16[480,256]{1,0:T(8,128)(2,1)}) %reduce-scatter.3.cloned.1.call-update) | async-done | bytes 245776 | tf_op jit(solution)/shard_map/reduce_scatter | solution.py:52
  50.8 4.0 slice.41
  54.9 0.2 convert_reduce_fusion
  55.0 0.3 fusion.26
  55.4 0.3 fusion.28
  55.7 76.9 %all-gather.4.cloned.1.call-done = bf16[7680,256]{1,0:T(8,128)(2,1)} async-done(((bf16[480,256]{1,0:T(8,128)(2,1)}), bf16[7680,256]{1,0:T(8,128)(2,1)}) %all-gather.4.cloned.1.call-update) | async-done | bytes 3932176 | tf_op jit(solution)/shard_map/all_gather | solution.py:55
  132.6 4.7 %fusion.20 = f32[256,256]{0,1:T(8,128)S(1)} fusion(bf16[7680,256]{1,0:T(8,128)(2,1)} %all-gather.4.cloned.1.call-done, bf16[256,6400]{1,0:T(8,128)(2,1)} %slice.41, bf16[256,1280]{1,0:T(8,128)(2,1)S(1)} %fusion.28), kind=kOutput, calls=%fused_computation.51 | convolution fusion | flops 1014497280 | bytes 8126464 | tf_op jit(solution)/shard_map/dot_general | solution.py:56
  137.4 0.1 multiply_convert_fusion
  137.6 0.8 copy.90
  138.3 0.0 reduce-scatter.5.cloned.1.call-start
  138.4 81.2 %all-gather.6.cloned.1.call-done = bf16[16,256,256]{2,1,0:T(8,128)(2,1)} async-done(((bf16[1,256,256]{2,1,0:T(8,128)(2,1)}), bf16[16,256,256]{2,1,0:T(8,128)(2,1)}) %all-gather.6.cloned.1.call-update) | async-done | bytes 2097168 | tf_op jit(solution)/shard_map/all_gather | solution.py:145
  219.6 2.5 conditional.2
  219.8 0.1 broadcast.193
  219.9 2.3 broadcast.194
  222.1 4.5 %convolution_convert_fusion.1 = bf16[16,65536]{1,0:T(8,128)(2,1)S(1)} fusion(f32[16,65536]{1,0:T(8,128)} %get-tuple-element.43, s32[16]{0:T(128)S(1)} %bitcast.171), kind=kOutput, calls=%fused_computation.50 | convolution fusion | flops 202375424 | bytes 6291520 | tf_op jit(solution)/shard_map/dot_general | solution.py:161
  226.6 2.0 convert_element_type.99
  228.7 0.0 all-gather.8.cloned.1.call-start
  228.7 126.3 %reduce-scatter.5.cloned.1.call-done = bf16[256,256]{1,0:T(8,128)(2,1)} async-done(((bf16[4096,256]{1,0:T(8,128)(2,1)}), bf16[256,256]{1,0:T(8,128)(2,1)}) %reduce-scatter.5.cloned.1.call-update) | async-done | bytes 131088 | tf_op jit(solution)/shard_map/reduce_scatter | solution.py:164
  355.0 1.3 collective-permute-start
  356.3 9.1 %collective-permute-done = bf16[256,256]{1,0:T(8,128)(2,1)S(1)} collective-permute-done((bf16[256,256]{1,0:T(8,128)(2,1)}, bf16[256,256]{1,0:T(8,128)(2,1)S(1)}, u32[]{:S(2)}, u32[]{:S(2)}) %collective-permute-start) | collective-permute-done | bytes 131104 | tf_op jit(solution)/shard_map/ppermute | solution.py:14
  365.4 0.1 copy.84
  365.5 0.1 fusion.32
  365.6 0.1 fusion.33
  365.7 0.8 copy.91
  366.5 32.6 %all-gather.8.cloned.1.call-done = bf16[256,2048]{1,0:T(8,128)(2,1)} async-done(((bf16[256,256]{1,0:T(8,128)(2,1)}), bf16[256,2048]{1,0:T(8,128)(2,1)}) %all-gather.8.cloned.1.call-update) | async-done | bytes 1048592 | tf_op jit(solution)/shard_map/all_gather | solution.py:178
  399.2 3.8 conditional.3
  399.2 3.8 convolution_convert_fusion
  403.1 0.9 select_bitcast_fusion
  403.9 0.5 copy-done.1
  (38 shorter events, 0.3 us)
Async XLA Ops:
  6.5 1.2 copy-start
  6.5 44.2 %reduce-scatter.3.cloned.1.call-start = ((), (), s32[]{:S(2)}) async-start(), calls=%async_computation.2 | async-start | bytes 2211840 | tf_op jit(solution)/shard_map/reduce_scatter | solution.py:52
  13.5 119.2 %all-gather.4.cloned.1.call-start = ((), (), s32[]{:S(2)}) async-start(), calls=%async_computation.3 | async-start | bytes 4177920 | tf_op jit(solution)/shard_map/all_gather | solution.py:55
  50.8 168.8 %all-gather.6.cloned.1.call-start = ((), (), s32[]{:S(2)}) async-start(), calls=%async_computation.4 | async-start | bytes 2228224 | tf_op jit(solution)/shard_map/all_gather | solution.py:145
  50.8 4.0 copy-start.2
  50.8 4.5 %copy-start.13 = (f32[1280]{0:T(1024)S(1)}, f32[1280]{0:T(1024)}, u32[]{:S(2)}) copy-start(f32[1280]{0:T(1024)} %param.16) | copy-start | bytes 15364
  55.6 81.8 %copy-start.14 = (f32[128]{0:T(128)S(1)}, f32[128]{0:T(128)}, u32[]{:S(2)}) copy-start(f32[128]{0:T(128)} %param.19) | copy-start | bytes 1540
  55.7 163.9 %copy-start.7 = (bf16[256,1024]{1,0:T(8,128)(2,1)S(1)}, bf16[256,1024]{1,0:T(8,128)(2,1)}, u32[]{:S(2)}) copy-start(bf16[256,1024]{1,0:T(8,128)(2,1)} %param.20) | copy-start | bytes 1572868
  55.7 163.9 %copy-start.15 = (f32[128]{0:T(128)S(1)}, f32[128]{0:T(128)}, u32[]{:S(2)}) copy-start(f32[128]{0:T(128)} %param.21) | copy-start | bytes 1540
  55.7 163.9 %copy-start.16 = (s32[16,1]{0,1:T(1,128)S(1)}, s32[16,1]{0,1:T(1,128)}, u32[]{:S(2)}) copy-start(s32[16,1]{0,1:T(1,128)} %param.24) | copy-start | bytes 196
  55.7 163.9 %copy-start.17 = (s32[16]{0:T(128)S(1)}, s32[16]{0:T(128)}, u32[]{:S(2)}) copy-start(s32[16]{0:T(128)} %param.25) | copy-start | bytes 196
  55.7 163.9 %copy-start.18 = (f32[8]{0:T(128)S(1)}, f32[8]{0:T(128)}, u32[]{:S(2)}) copy-start(f32[8]{0:T(128)} %param.22) | copy-start | bytes 100
  138.3 216.7 %reduce-scatter.5.cloned.1.call-start = ((), (), s32[]{:S(2)}) async-start(), calls=%async_computation.5 | async-start | bytes 2228224 | tf_op jit(solution)/shard_map/reduce_scatter | solution.py:164
  222.1 4.5 %copy-start.5 = (bf16[256,1024]{1,0:T(8,128)(2,1)}, bf16[256,1024]{1,0:T(8,128)(2,1)S(1)}, u32[]{:S(2)}) copy-start(bf16[256,1024]{1,0:T(8,128)(2,1)S(1)} %get-tuple-element.44) | copy-start | bytes 1572868
  228.7 170.5 %all-gather.8.cloned.1.call-start = ((), (), s32[]{:S(2)}) async-start(), calls=%async_computation.6 | async-start | bytes 1179648 | tf_op jit(solution)/shard_map/all_gather | solution.py:178
  355.0 10.3 %collective-permute-start = (bf16[256,256]{1,0:T(8,128)(2,1)}, bf16[256,256]{1,0:T(8,128)(2,1)S(1)}, u32[]{:S(2)}, u32[]{:S(2)}) collective-permute-start(bf16[256,256]{1,0:T(8,128)(2,1)} %reduce-scatter.5.cloned.1.call-done), channel_id=1, source_target_pairs={{128,0},{129,1},{130,2},{131,3},{132,4},{133,5},{134,6},{135,7},{1... | collective-permute-start | bytes 393224 | tf_op jit(solution)/shard_map/ppermute | solution.py:14
  399.2 3.9 copy-start.6
  403.0 1.4 copy-start.1
Sparse Core Ops, SparseCore 0:
  13.6 37.1 reduce-scatter.2
  52.7 79.9 all-gather.3
  138.5 81.0 all-gather.5
  228.8 126.1 reduce-scatter.4
  366.7 32.4 all-gather.7

commit v2 on v1

v2 whole, which is shorter than its diff:
```python
import math

import jax
import jax.numpy as jnp
from jax import lax
from jax.experimental import pallas as pl
from jax.experimental.pallas import tpu as pltpu
from jax.sharding import PartitionSpec as P

MESH = pl.DeviceIdType.MESH
F32, BF16 = jnp.float32, jnp.bfloat16
epsilon = 1e-05

VIN, VD, HD = 7680, 1280, 128
ROWS = 256
WROWS = 480
WHALF = WROWS // 2
HALF = ROWS // 2
INV = 1.0 / math.sqrt(HD)

RIGHT, LEFT = 0, 1

_sizes = dict(
    wsib=2, wy=6, qg=1,
    wz=4, wzf=2, wx=16, wxf=8,
    kz=4, kzf=2, kx=16, kxf=8,
    share=16, gsib=16,
    rxo=8, rx=16, rzo=2, rz=4,
    pgx=1, pgy=6, pgs=2, dq=2,
)
BASE = {}
_total = 0
for _name, _size in _sizes.items():
    BASE[_name] = _total
    _total += _size
PLACES = _total


def gray(k):
    return k + (k // 2) * (1 - 2 * (k % 2))


def nt(a, b):
    return lax.dot_general(a, b, (((1,), (1,)), ((), ())), preferred_element_type=F32)


def tn(a, b):
    return lax.dot_general(a, b, (((0,), (0,)), ((), ())), preferred_element_type=F32)


def kernel(
    img_hbm, ngain, proj_hbm, kv_hbm, kgain, q_hbm, qgain, hgate, cot_hbm, block_image, image_len,
    out,
    img, proj, kvall, queries, cot,
    wsend, wown, wsib, wys, wyr, wg,
    projf, kvb, qgb, dqbuf, dqo, dqin,
    gsend, gown, gsib, rsb, rxo_in, rx_in, rzo_in, rz_in, ztot,
    pgbuf, acc,
    ssem, rsem, lsem,
):
    g = lax.axis_index("group")
    s = lax.axis_index("seq")
    m = lax.axis_index("mp")
    z, x = s // 4, s % 4
    y, c = m // 2, m % 2
    p = gray(z)
    other = 1 - c

    xs = [x, (x + 1) % 4, (x + 3) % 4, (x + 2) % 4]
    zs = [z, gray((p + 1) % 4), gray((p + 3) % 4), gray((p + 2) % 4)]

    sib = (g, s, 2 * y + other)
    ydev = [None] + [(g, s, 2 * ((y + d) % 4) + c) for d in (1, 2, 3)]
    xdev = [(g, z * 4 + xs[1], m), (g, z * 4 + xs[2], m)]
    zdev = [(g, zs[1] * 4 + x, m), (g, zs[2] * 4 + x, m)]
    across = (1 - g, s, m)
    across_sib = (1 - g, s, 2 * y + other)

    def rc(place, src, dst, dev):
        return pltpu.make_async_remote_copy(
            src_ref=src, dst_ref=dst, send_sem=ssem.at[place], recv_sem=rsem.at[place],
            device_id=dev, device_id_type=MESH,
        )

    def send(place, src, dst, dev):
        copy = rc(place, src, dst, dev)
        copy.start()
        return copy

    def left(place, ref):
        rc(place, ref, ref, sib).wait_send()

    def arrived(place, dst):
        rc(place, dst, dst, sib).wait_recv()

    local = {}

    def load(name, src, dst):
        copy = pltpu.make_async_copy(src, dst, lsem.at[len(local)])
        local[name] = copy
        return copy

    def strip(par, kind, yy):
        return load(
            ("kv", len(local)),
            kv_hbm.at[:, pl.ds(pl.multiple_of((2 * yy + par) * 256 + kind * 128, 128), 128)],
            kvall.at[par, kind, :, yy * 128:(yy + 1) * 128],
        )

    proj_load = load("proj", proj_hbm, proj)
    proj_load.start()
    kv_sib = [strip(g, other, yy) for yy in range(4)]
    for copy in kv_sib:
        copy.start()
    kv_own = [strip(g, c, yy) for yy in range(4)]
    for copy in kv_own:
        copy.start()
    q_load = load("q", q_hbm, queries)
    q_load.start()
    cot_load = load("cot", cot_hbm, cot)
    cot_load.start()
    img_load = load("img", img_hbm, img)
    img_load.start()
    kv_rest = [strip(1 - g, kind, yy) for kind in range(2) for yy in range(4)]

    @pl.when(g == 0)
    def _():
        for copy in kv_rest:
            copy.start()

    barrier = pltpu.get_barrier_semaphore()
    for dev in [sib, *ydev[1:], *xdev, *zdev, across, across_sib]:
        pl.semaphore_signal(barrier, inc=1, device_id=dev, device_id_type=MESH)

    proj_load.wait()
    for copy in kv_sib:
        copy.wait()

    def share_of(r, kind):
        return jnp.dot(
            proj[r * WHALF:(r + 1) * WHALF, :], kvall[g, kind], preferred_element_type=F32
        )

    wsend[0] = share_of(0, other).astype(BF16)
    pl.semaphore_wait(barrier, 10)
    send(BASE["wsib"], wsend.at[0], wsib.at[0], sib)
    wsend[1] = share_of(1, other).astype(BF16)
    send(BASE["wsib"] + 1, wsend.at[1], wsib.at[1], sib)
    for copy in kv_own:
        copy.wait()

    def rows_of(block, r):
        return pl.ds(pl.multiple_of(block * WROWS + r * WHALF, 16), WHALF)

    def wloc(block, r):
        return wg.at[rows_of(block, r), :]

    def kloc(block, r):
        return kvb.at[c, block, r * HALF:(r + 1) * HALF, :]

    def block_of(xrel, zrel):
        return zs[zrel] * 4 + xs[xrel]

    def gather(kind, loc):
        zb, zf = BASE[kind + "z"], BASE[kind + "zf"]
        xb, xf = BASE[kind + "x"], BASE[kind + "xf"]

        def z_own(r):
            ref = loc(block_of(0, 0), r)
            for way in (RIGHT, LEFT):
                send(zb + way * 2 + r, ref, ref, zdev[way])

        def x_direct(zrel, r):
            ref = loc(block_of(0, zrel), r)
            for way in (RIGHT, LEFT):
                send(xb + (way * 4 + zrel) * 2 + r, ref, ref, xdev[way])

        def z_first(way, r):
            zrel = 2 if way == RIGHT else 1
            ref = loc(block_of(0, zrel), r)
            arrived(zb + way * 2 + r, ref)
            if r == way:
                send(zf + way, ref, ref, zdev[way])
            x_direct(zrel, r)

        def z_second(way):
            arrived(zf + way, loc(block_of(0, 3), way))
            x_direct(3, way)

        def x_first(way, zrel, r):
            xrel = 2 if way == RIGHT else 1
            ref = loc(block_of(xrel, zrel), r)
            arrived(xb + (way * 4 + zrel) * 2 + r, ref)
            if r == way:
                send(xf + way * 4 + zrel, ref, ref, xdev[way])

        def x_second(way, zrel):
            arrived(xf + way * 4 + zrel, loc(block_of(3, zrel), way))

        return z_own, x_direct, z_first, z_second, x_first, x_second

    w_z_own, w_x_direct, w_z_first, w_z_second, w_x_first, w_x_second = gather("w", wloc)

    wown[0] = share_of(0, c)
    wown[1] = share_of(1, c)

    def to_y(r):
        arrived(BASE["wsib"] + r, wsib.at[r])
        for yy in range(4):
            cols = slice(yy * 128, (yy + 1) * 128)
            wys[r, yy] = (wown[r, :, cols] + wsib[r, :, cols].astype(F32)).astype(BF16)
        for d in (1, 2, 3):
            send(BASE["wy"] + r * 3 + d - 1, wys.at[r, (y + d) % 4], wyr.at[r, d - 1], ydev[d])

    def own_w(r):
        total = wys[r, y].astype(F32)
        for d in (1, 2, 3):
            arrived(BASE["wy"] + r * 3 + d - 1, wyr.at[r, d - 1])
            total = total + wyr[r, d - 1].astype(F32)
        wg[rows_of(s, r), :] = total.astype(BF16)
        w_z_own(r)
        w_x_direct(0, r)

    to_y(0)
    to_y(1)
    own_w(0)
    own_w(1)

    q_load.wait()
    cot_load.wait()

    @pl.when(c == g)
    def _():
        for h in range(8):
            cols = slice(h * 128, (h + 1) * 128)
            rows = slice((h % 4) * 16, (h % 4 + 1) * 16)
            wide = queries[:, cols].astype(F32)
            scale = lax.rsqrt(jnp.mean(wide * wide, axis=-1, keepdims=True) + epsilon)
            low = (wide * scale * qgain[...]).astype(BF16)
            qgb[h // 4, 0, :, rows, :] = low.reshape(16, 16, HD)
            gate = jnp.tanh(jnp.full((1, HD), hgate[h], F32))
            grad = (cot[:, cols].astype(F32) * gate).astype(BF16)
            qgb[h // 4, 1, :, rows, :] = grad.reshape(16, 16, HD)
        send(BASE["qg"], qgb.at[other], qgb.at[other], sib)

    img_load.wait()
    for part in range(4):
        rows = slice(part * 64, (part + 1) * 64)
        lead = img[rows, :VD].astype(F32)
        center = jnp.mean(lead, axis=-1, keepdims=True)
        spread = jnp.mean((lead - center) ** 2, axis=-1, keepdims=True)
        img[rows, :VD] = ((lead - center) * lax.rsqrt(spread + epsilon) * ngain[...]).astype(BF16)

    for r in (0, 1):
        w_z_first(RIGHT, r)
        w_z_first(LEFT, r)
    for r in (0, 1):
        w_x_first(RIGHT, 0, r)
        w_x_first(LEFT, 0, r)
    w_z_second(RIGHT)
    w_z_second(LEFT)
    for zrel in (1, 2, 3):
        for r in (0, 1):
            w_x_first(RIGHT, zrel, r)
            w_x_first(LEFT, zrel, r)
    for zrel in range(4):
        w_x_second(RIGHT, zrel)
        w_x_second(LEFT, zrel)

    projf[...] = jnp.zeros((ROWS, HD), F32)

    @pl.loop(0, 4)
    def _(part):
        cols = pl.ds(pl.multiple_of(part * 1920, 128), 1920)
        projf[...] += jnp.dot(img[:, cols], wg[cols, :], preferred_element_type=F32)

    made = projf[...]
    key_scale = lax.rsqrt(jnp.mean(made * made, axis=-1, keepdims=True) + epsilon)
    kvb[c, s] = jnp.where(c == 0, made * key_scale * kgain[...], made).astype(BF16)

    k_z_own, k_x_direct, k_z_first, k_z_second, k_x_first, k_x_second = gather("k", kloc)
    k_z_own(0)
    k_z_own(1)
    k_x_direct(0, 0)
    k_x_direct(0, 1)

    def hand_over(it, block):
        send(BASE["share"] + it, kvb.at[c, block], kvb.at[c, block], sib)

    @pl.when(c != g)
    def _():
        arrived(BASE["qg"], qgb.at[c])

    def image_of(it):
        xx = (x + gray(it // 4)) % 4
        zz = gray((p + gray(it % 4)) % 4)
        return zz * 4 + xx

    def finish(it):
        xrel, zrel = it // 4, it % 4
        arrived(BASE["gsib"] + it, gsib.at[it])
        total = gown[it] + gsib[it].astype(F32)
        gown[it] = total
        rsb[it] = total.astype(BF16)

        def go(way, r, base, dst):
            send(base, rsb.at[it, r * HALF:(r + 1) * HALF, :], dst, xdev[way])

        @pl.when(xrel == 1)
        def _():
            go(RIGHT, 1, BASE["rx"] + (RIGHT * 4 + zrel) * 2 + 1, rx_in.at[RIGHT, zrel, 1])

        @pl.when(xrel == 2)
        def _():
            go(LEFT, 0, BASE["rx"] + (LEFT * 4 + zrel) * 2 + 0, rx_in.at[LEFT, zrel, 0])

        @pl.when(xrel == 3)
        def _():
            go(RIGHT, 0, BASE["rxo"] + RIGHT * 4 + zrel, rxo_in.at[RIGHT, zrel])
            go(LEFT, 1, BASE["rxo"] + LEFT * 4 + zrel, rxo_in.at[LEFT, zrel])

    def before(k):
        xrel, zrel = k // 4, k % 4
        if xrel == 0:
            if zrel == 1:
                for r in (0, 1):
                    k_z_first(RIGHT, r)
                    k_z_first(LEFT, r)
            if zrel == 3:
                k_z_second(RIGHT)
                k_z_second(LEFT)
        elif xrel == 1:
            for r in (0, 1):
                k_x_first(LEFT, zrel, r)
                k_x_first(RIGHT, zrel, r)
        elif xrel == 3:
            k_x_second(RIGHT, zrel)
            k_x_second(LEFT, zrel)
        hand_over(k, block_of(xrel, zrel))

    @pl.loop(0, 16)
    def _(it):
        for k in range(16):
            @pl.when(it == k)
            def _(k=k):
                before(k)

        i = image_of(it)
        first, last, seen = i * 0, i * 0, i * 0
        for b in range(16):
            hit = (block_image[b, 0] == i).astype(jnp.int32)
            first = first + b * hit * (1 - seen)
            last = last + (b - last) * hit
            seen = seen + hit * (1 - seen)
        use0 = seen > 0
        use1 = last > first
        at0, at1 = first, last
        zero = jnp.zeros((64, HD), BF16)
        low = jnp.concatenate(
            [jnp.where(use0, qgb[c, 0, at0], zero), jnp.where(use1, qgb[c, 0, at1], zero)], axis=0
        )
        grad = jnp.concatenate(
            [jnp.where(use0, qgb[c, 1, at0], zero), jnp.where(use1, qgb[c, 1, at1], zero)], axis=0
        )
        arrived(BASE["share"] + it, kvb.at[other, i])
        keys, values = kvb[0, i], kvb[1, i]
        scores = nt(keys, low) * INV
        usable = lax.broadcasted_iota(jnp.int32, (ROWS, HD), 0) < image_len[i]
        raised = jnp.where(usable, jnp.exp(scores), 0.0)
        weights = raised / jnp.sum(raised, axis=0, keepdims=True)
        weight_grads = nt(values, grad)
        inner = jnp.sum(weights * weight_grads, axis=0, keepdims=True)
        score_grads = (weights * (weight_grads - inner) * INV).astype(BF16)
        key_grads = jnp.dot(score_grads, low, preferred_element_type=F32)
        value_grads = jnp.dot(weights.astype(BF16), grad, preferred_element_type=F32)
        gown[it] = jnp.where(c == 0, key_grads, value_grads)
        gsend[it] = jnp.where(c == 0, value_grads, key_grads).astype(BF16)
        send(BASE["gsib"] + it, gsend.at[it], gsib.at[it], sib)
        dqbuf[i] = tn(score_grads, keys).astype(BF16).reshape(2, 64, HD)

        @pl.when(it > 0)
        def _():
            finish(it - 1)

    finish(15)

    @pl.loop(0, 16)
    def _(b):
        mine = block_image[b, 0]
        slot = b * 0
        for bb in range(16):
            hit = ((bb < b) & (block_image[bb, 0] == mine)).astype(jnp.int32)
            slot = slot + hit * (1 - slot)
        dqo[b] = dqbuf[mine, slot]

    @pl.when(g == 0)
    def _():
        send(BASE["dq"] + c, dqo, dqin.at[c], (1, s, 2 * y))

    @pl.when((g == 1) & (c == 0))
    def _():
        send(BASE["dq"], dqo, dqin.at[0], sib)

    @pl.when((g == 1) & (c == 1))
    def _():
        dqin[1] = dqo[...]

    def half(r):
        return slice(r * HALF, (r + 1) * HALF)

    for zrel in range(4):
        for way in (RIGHT, LEFT):
            it = (1 if way == RIGHT else 2) * 4 + zrel
            r = way
            arrived(BASE["rxo"] + way * 4 + zrel, rxo_in.at[way, zrel])
            rsb[it, half(r)] = (gown[it, half(r)] + rxo_in[way, zrel].astype(F32)).astype(BF16)
            send(
                BASE["rx"] + (way * 4 + zrel) * 2 + r, rsb.at[it, half(r)], rx_in.at[way, zrel, r],
                xdev[way],
            )

    def x_total(zrel, r):
        total = gown[zrel, half(r)]
        for way in (RIGHT, LEFT):
            arrived(BASE["rx"] + (way * 4 + zrel) * 2 + r, rx_in.at[way, zrel, r])
            total = total + rx_in[way, zrel, r].astype(F32)
        return total

    for r in (0, 1):
        ztot[3, half(r)] = x_total(3, r).astype(BF16)
        send(BASE["rzo"] + r, ztot.at[3, half(r)], rzo_in.at[r], zdev[r])
    for way in (RIGHT, LEFT):
        zrel = 1 if way == RIGHT else 2
        r = 1 - way
        ztot[zrel, half(r)] = x_total(zrel, r).astype(BF16)
        send(BASE["rz"] + way * 2 + r, ztot.at[zrel, half(r)], rz_in.at[way, r], zdev[way])
    for way in (RIGHT, LEFT):
        zrel = 1 if way == RIGHT else 2
        r = way
        total = x_total(zrel, r)
        arrived(BASE["rzo"] + way, rzo_in.at[way])
        ztot[zrel, half(r)] = (total + rzo_in[way].astype(F32)).astype(BF16)
        send(BASE["rz"] + way * 2 + r, ztot.at[zrel, half(r)], rz_in.at[way, r], zdev[way])
    for r in (0, 1):
        total = x_total(0, r)
        for way in (RIGHT, LEFT):
            arrived(BASE["rz"] + way * 2 + r, rz_in.at[way, r])
            total = total + rz_in[way, r].astype(F32)
        raw = projf[half(r)]
        scale = lax.rsqrt(jnp.mean(raw * raw, axis=-1, keepdims=True) + epsilon)
        scaled = total * kgain[...]
        back = scale * (
            scaled - raw * (scale * scale) * jnp.mean(scaled * raw, axis=-1, keepdims=True)
        )
        pgbuf[g, c, y, half(r)] = jnp.where(c == 0, back, total).astype(BF16)

    @pl.when(g == 1)
    def _():
        copy = send(BASE["pgx"], pgbuf.at[1, c, y], pgbuf.at[1, c, y], across)
        for half_of in range(2):
            @pl.when((c == 0) | (half_of == 0))
            def _():
                arrived(BASE["dq"] + half_of, dqin.at[half_of])
        for h in range(8):
            cols = slice(h * 128, (h + 1) * 128)
            rows = slice((h % 4) * 16, (h % 4 + 1) * 16)
            d = dqin[h // 4, :, rows, :].reshape(ROWS, HD).astype(F32) * qgain[...]
            wide = queries[:, cols].astype(F32)
            scale = lax.rsqrt(jnp.mean(wide * wide, axis=-1, keepdims=True) + epsilon)
            res = scale * (d - wide * (scale * scale) * jnp.mean(d * wide, axis=-1, keepdims=True))
            out[0, :, cols] = res.astype(BF16)
        copy.wait_send()

    @pl.when(g == 0)
    def _():
        mine = []
        for par in range(2):
            if par == 1:
                arrived(BASE["pgx"], pgbuf.at[1, c, y])
            for d in (1, 2, 3):
                ref = pgbuf.at[par, c, y]
                mine.append(send(BASE["pgy"] + par * 3 + d - 1, ref, ref, ydev[d]))
            for d in (1, 2, 3):
                arrived(BASE["pgy"] + par * 3 + d - 1, pgbuf.at[par, c, (y + 4 - d) % 4])
            ref = pgbuf.at[par, c]
            mine.append(send(BASE["pgs"] + par, ref, ref, sib))
            if par == 1:
                for copy in kv_rest:
                    copy.wait()

            def term(kind):
                cat = jnp.concatenate([pgbuf[par, kind, yy] for yy in range(4)], axis=1)
                return nt(cat, kvall[par, kind])

            if par == 0:
                acc[...] = term(c)
            else:
                acc[...] += term(c)
            arrived(BASE["pgs"] + par, pgbuf.at[par, other])
            if par == 0:
                acc[...] += term(other)
            else:
                out[0] = (acc[...] + term(other)).astype(BF16)
        for copy in mine:
            copy.wait_send()

    for name, piece in (
        ("wsib", wsend.at[0]),
        ("wy", wys.at[0, 0]),
        ("wz", wg.at[0:WHALF, :]),
        ("wzf", wg.at[0:WHALF, :]),
        ("wx", wg.at[0:WHALF, :]),
        ("wxf", wg.at[0:WHALF, :]),
        ("kz", kvb.at[0, 0, 0:HALF, :]),
        ("kzf", kvb.at[0, 0, 0:HALF, :]),
        ("kx", kvb.at[0, 0, 0:HALF, :]),
        ("kxf", kvb.at[0, 0, 0:HALF, :]),
        ("share", kvb.at[0, 0]),
        ("rx", rsb.at[0, 0:HALF, :]),
        ("rxo", rsb.at[0, 0:HALF, :]),
        ("rzo", ztot.at[0, 0:HALF, :]),
        ("rz", ztot.at[0, 0:HALF, :]),
    ):
        for k in range(_sizes[name]):
            left(BASE[name] + k, piece)

    for it in range(16):
        left(BASE["gsib"] + it, gsend.at[it])
    @pl.when(c == g)
    def _():
        left(BASE["qg"], qgb.at[other])

    @pl.when(g == 0)
    def _():
        left(BASE["dq"] + c, dqo)

    @pl.when((g == 1) & (c == 0))
    def _():
        left(BASE["dq"], dqo)


def per_device(
    image_states, norm_gain, proj_weight, kv_weight, key_gain, queries, query_gain, head_gate,
    cotangent, block_image, image_len,
):
    anywhere = pl.BlockSpec(memory_space=pl.ANY)
    vmem = pl.BlockSpec(memory_space=pltpu.VMEM)
    smem = pl.BlockSpec(memory_space=pltpu.SMEM)
    V = pltpu.VMEM
    scratch = [
        V((ROWS, VIN), BF16),
        V((WROWS, 1024), BF16),
        V((2, 2, 1024, 512), BF16),
        V((ROWS, 1024), BF16),
        V((ROWS, 1024), BF16),
        V((2, WHALF, 512), BF16),
        V((2, WHALF, 512), F32),
        V((2, WHALF, 512), BF16),
        V((2, 4, WHALF, HD), BF16),
        V((2, 3, WHALF, HD), BF16),
        V((VIN, HD), BF16),
        V((ROWS, HD), F32),
        V((2, 16, ROWS, HD), BF16),
        V((2, 2, 16, 64, HD), BF16),
        V((16, 2, 64, HD), BF16),
        V((16, 64, HD), BF16),
        V((2, 16, 64, HD), BF16),
        V((16, ROWS, HD), BF16),
        V((16, ROWS, HD), F32),
        V((16, ROWS, HD), BF16),
        V((16, ROWS, HD), BF16),
        V((2, 4, HALF, HD), BF16),
        V((2, 4, 2, HALF, HD), BF16),
        V((2, HALF, HD), BF16),
        V((2, 2, HALF, HD), BF16),
        V((4, ROWS, HD), BF16),
        V((2, 2, 4, ROWS, HD), BF16),
        V((ROWS, 1024), F32),
        pltpu.SemaphoreType.DMA((PLACES,)),
        pltpu.SemaphoreType.DMA((PLACES,)),
        pltpu.SemaphoreType.DMA((24,)),
    ]
    return pl.pallas_call(
        kernel,
        out_shape=jax.ShapeDtypeStruct((1, ROWS, 1024), BF16),
        in_specs=[
            anywhere, vmem, anywhere, anywhere, vmem, anywhere, vmem, smem, anywhere, smem, smem,
        ],
        out_specs=vmem,
        scratch_shapes=scratch,
        compiler_params=pltpu.CompilerParams(
            collective_id=0, has_side_effects=True, vmem_limit_bytes=48 * 2**20
        ),
    )(
        image_states.reshape(ROWS, VIN), norm_gain.reshape(1, VD), proj_weight, kv_weight,
        key_gain.reshape(1, HD), queries, query_gain.reshape(1, HD), head_gate, cotangent,
        block_image, image_len,
    )


def solution(mesh):
    placed = (
        P("seq", None, None), P(), P("seq", "mp"), P("mp", None), P(), P("seq", "mp"), P(),
        P("mp"), P("seq", "mp"), P("seq", None), P(),
    )
    return jax.shard_map(
        per_device, mesh=mesh, in_specs=placed, out_specs=P("group", "seq", "mp"), check_vma=False
    )
```

time: 412 us -> 115 us (0.28)
  waiting for transfers between devices: 363 us -> 0 us
  Pallas kernels: 0 us -> 105 us
  matrix products: 18.8 us -> 0 us
  between operations: 13.4 us -> 0.02 us
    all_gather x3 -> x0, waiting for transfers between devices: 191 us -> none  [the longest x1 81.2 us: per_device(): gathered = lax.all_gather(keyval, 'seq', axis=0, tiled=True)]
    reduce_scatter x2 -> x0, waiting for transfers between devices: 164 us -> none  [the longest x1 126 us: per_device(): lax.psum_scatter(summed.reshape(lax.axis_size('seq') * own_rows, kv_width...]
    pallas_call x0 -> x1, Pallas kernels: none -> 105 us  [per_device(): pl.pallas_call(kernel, out_shape=jax.ShapeDtypeStruct((1, ROWS, 1024), BF...]
    dot_general x4 -> x0, matrix products: 18.8 us -> none  [the longest x1 5.69 us: per_device(): jnp.dot(proj_weight, kv_weight, preferred_element_type=jnp.float32)]
    ppermute x1 -> x0, waiting for transfers between devices: 9.06 us -> none  [passed_along(): return lax.ppermute(x, axis, pairs)]
    unnamed x24 -> x16, local copies, waits for them, and re-layouts: 1.78 us -> 7.43 us
  transfers between devices with their start and end apart: 6 -> 0, of which waited for: 6 -> 0; matrix products, arithmetic and copies ran while one was open for 1% -> 0% of each run, Pallas kernels for 0% -> 0%
where the time goes in v2:
time: 115 us; the launch traced here: 113 us
  Pallas kernels  105 us (91%)
  local copies, waits for them, and re-layouts  8.13 us (7%)
    pallas_call x1, Pallas kernels, per_device(): pl.pallas_call(kernel, out_shape=jax.ShapeDtypeStruct((1, ROWS, 1024), BF...  105 us
    unnamed x16, local copies, waits for them, and re-layouts  7.43 us

profile of v2, /device:TPU:1, one launch (start us, length us, event | category | flops | bytes accessed | tf_op | source)
XLA Modules:
  0.0 113.5 jit_solution(913783705504089252)
XLA Ops:
  0.0 0.7 reshape.13.ngain
  0.7 0.7 copy.12.block_image
  1.4 0.0 copy-start
  1.4 1.2 %copy-done = bf16[480,1024]{1,0:T(8,128)(2,1)S(1)} copy-done((bf16[480,1024]{1,0:T(8,128)(2,1)S(1)}, bf16[480,1024]{1,0:T(8,128)(2,1)}, u32[]{:S(2)}) %copy-start) | copy-done | bytes 983064
  2.6 0.0 copy-start.1
  2.6 1.0 copy-done.1
  3.7 0.0 copy-start.2
  3.7 1.0 copy-done.2
  4.7 0.0 copy-start.3
  4.7 0.7 copy-done.3
  5.4 0.0 copy-start.4
  5.4 0.7 copy-done.4
  6.0 0.0 copy-start.5
  6.0 0.7 copy-done.5
  6.7 0.0 copy-start.6
  6.7 0.7 copy-done.6
  7.3 105.3 %shard_map.109 = bf16[1,256,1024]{2,1,0:T(8,128)(2,1)S(1)} custom-call(bf16[256,7680]{1,0:T(8,128)(2,1)} %bitcast.5, f32[1,1280]{1,0:T(1,128)S(1)} %reshape.13.ngain, bf16[480,1024]{1,0:T(8,128)(2,1)S(1)} %copy-done, bf16[1024,2048]{1,0:T(8,128)(2,1)} %kv_hbm.1, f32[1,128]{1,0:T(1,128)S(1)} %bitcast.3, bf16[256,1024]{1,0:T(8,128)(2,1)S(1)} %copy-done.1, ...), custom_call_target="tpu_custom_call" | custom-call | tf_op jit(solution)/shard_map/pallas_call | solution.py:583
  112.7 0.8 copy.14
Async XLA Ops:
  1.4 1.2 %copy-start = (bf16[480,1024]{1,0:T(8,128)(2,1)S(1)}, bf16[480,1024]{1,0:T(8,128)(2,1)}, u32[]{:S(2)}) copy-start(bf16[480,1024]{1,0:T(8,128)(2,1)} %proj_hbm.1) | copy-start | bytes 2949124
  2.6 1.0 copy-start.1
  3.7 1.0 copy-start.2
  4.7 0.7 copy-start.3
  5.4 0.7 copy-start.4
  6.0 0.7 copy-start.5
  6.7 0.7 copy-start.6

commit v3 on v2

v3 whole, which is shorter than its diff:
```python
import math

import jax
import jax.numpy as jnp
from jax import lax
from jax.experimental import pallas as pl
from jax.experimental.pallas import tpu as pltpu
from jax.sharding import PartitionSpec as P

MESH = pl.DeviceIdType.MESH
F32, BF16 = jnp.float32, jnp.bfloat16
epsilon = 1e-05

VIN, VD, HD = 7680, 1280, 128
ROWS = 256
WROWS = 480
WHALF = WROWS // 2
HALF = ROWS // 2
INV = 1.0 / math.sqrt(HD)

RIGHT, LEFT = 0, 1

_sizes = dict(
    wsib=2, wy=6, route=40,
    wz=6, wx=16, wxf=8,
    share=1, gsib=1,
    pgx=1, pgy=6, pgs=8, back=32,
)
BASE = {}
_total = 0
for _name, _size in _sizes.items():
    BASE[_name] = _total
    _total += _size
PLACES = _total


def gray(k):
    return k + (k // 2) * (1 - 2 * (k % 2))


def nt(a, b):
    return lax.dot_general(a, b, (((1,), (1,)), ((), ())), preferred_element_type=F32)


def tn(a, b):
    return lax.dot_general(a, b, (((0,), (0,)), ((), ())), preferred_element_type=F32)


def kernel(
    img_hbm, ngain_hbm, proj_hbm, kv_hbm, kgain_hbm, q_hbm, qgain_hbm, hgate_hbm, cot_hbm,
    block_image_hbm, image_len_hbm,
    out,
    ngain, kgain, qgain, hgate, block_image, image_len,
    img, proj, kvall, queries, cot,
    wsend, wown, wsib, wys, wyr, wg,
    projf, kvb, qgb, qsend, qin, dqout, dqin, dqs,
    gmade, gsib,
    pgbuf, acc,
    ssem, rsem, lsem,
):
    g = lax.axis_index("group")
    s = lax.axis_index("seq")
    m = lax.axis_index("mp")
    z, x = s // 4, s % 4
    y, c = m // 2, m % 2
    p = gray(z)
    other = 1 - c

    xs = [x, (x + 1) % 4, (x + 3) % 4, (x + 2) % 4]
    zs = [z, gray((p + 1) % 4), gray((p + 3) % 4), gray((p + 2) % 4)]

    sib = (g, s, 2 * y + other)
    ydev = [None] + [(g, s, 2 * ((y + d) % 4) + c) for d in (1, 2, 3)]
    xdev = [(g, z * 4 + xs[1], m), (g, z * 4 + xs[2], m)]
    xfar = (g, z * 4 + xs[3], m)
    zdev = [(g, zs[k] * 4 + x, m) for k in (1, 2, 3)]
    across = (1 - g, s, m)

    def rc(place, src, dst, dev):
        return pltpu.make_async_remote_copy(
            src_ref=src, dst_ref=dst, send_sem=ssem.at[place], recv_sem=rsem.at[place],
            device_id=dev, device_id_type=MESH,
        )

    def send(place, src, dst, dev):
        copy = rc(place, src, dst, dev)
        copy.start()
        return copy

    def left(place, ref):
        rc(place, ref, ref, sib).wait_send()

    def arrived(place, dst):
        rc(place, dst, dst, sib).wait_recv()

    local = {}

    def load(name, src, dst):
        copy = pltpu.make_async_copy(src, dst, lsem.at[len(local)])
        local[name] = copy
        return copy

    def strip(par, kind, yy):
        return load(
            ("kv", len(local)),
            kv_hbm.at[:, pl.ds(pl.multiple_of((2 * yy + par) * 256 + kind * 128, 128), 128)],
            kvall.at[par, kind, :, yy * 128:(yy + 1) * 128],
        )

    proj_load = load("proj", proj_hbm, proj)
    proj_load.start()
    kv_sib = [strip(g, other, yy) for yy in range(4)]
    for copy in kv_sib:
        copy.start()
    kv_own = [strip(g, c, yy) for yy in range(4)]
    for copy in kv_own:
        copy.start()
    q_load = load("q", q_hbm, queries)
    q_load.start()
    cot_load = load("cot", cot_hbm, cot)
    cot_load.start()
    img_load = load("img", img_hbm, img)
    img_load.start()
    small = [
        load("ngain", ngain_hbm, ngain),
        load("kgain", kgain_hbm, kgain),
        load("qgain", qgain_hbm, qgain),
        load("hgate", hgate_hbm, hgate),
        load("block_image", block_image_hbm, block_image),
        load("image_len", image_len_hbm, image_len),
    ]
    for copy in small:
        copy.start()
    kv_rest = [strip(1 - g, kind, yy) for kind in range(2) for yy in range(4)]

    @pl.when(g == 0)
    def _():
        for copy in kv_rest:
            copy.start()

    barrier = pltpu.get_barrier_semaphore()
    for dev in ydev[1:]:
        pl.semaphore_signal(barrier, inc=1, device_id=dev, device_id_type=MESH)

    @pl.loop(1, 64)
    def _(k):
        at = (g * 32 + s * 2 + c + k) % 64
        dev = (at // 32, (at // 2) % 16, 2 * y + at % 2)
        pl.semaphore_signal(barrier, inc=1, device_id=dev, device_id_type=MESH)

    proj_load.wait()
    for copy in kv_sib:
        copy.wait()

    def share_of(r, kind):
        return jnp.dot(
            proj[r * WHALF:(r + 1) * WHALF, :], kvall[g, kind], preferred_element_type=F32
        )

    wsend[0] = share_of(0, other).astype(BF16)
    pl.semaphore_wait(barrier, 66)
    send(BASE["wsib"], wsend.at[0], wsib.at[0], sib)
    wsend[1] = share_of(1, other).astype(BF16)
    send(BASE["wsib"] + 1, wsend.at[1], wsib.at[1], sib)
    for copy in kv_own:
        copy.wait()

    def rows_of(block, r):
        return pl.ds(pl.multiple_of(block * WROWS + r * WHALF, 16), WHALF)

    def wloc(block, r):
        return wg.at[rows_of(block, r), :]

    def block_of(xrel, zrel):
        return zs[zrel] * 4 + xs[xrel]

    def gather(kind, loc):
        zb, xb, xf = BASE[kind + "z"], BASE[kind + "x"], BASE[kind + "xf"]

        def z_own(r):
            ref = loc(block_of(0, 0), r)
            for k in (1, 2, 3):
                send(zb + (k - 1) * 2 + r, ref, ref, zdev[k - 1])

        def x_direct(zrel, r):
            ref = loc(block_of(0, zrel), r)
            for way in (RIGHT, LEFT):
                send(xb + (way * 4 + zrel) * 2 + r, ref, ref, xdev[way])
            if zrel == 3:
                send(xf + r * 4 + zrel, ref, ref, xfar)

        def z_in(zrel, r):
            k = (0, 2, 1, 3)[zrel]
            arrived(zb + (k - 1) * 2 + r, loc(block_of(0, zrel), r))
            x_direct(zrel, r)

        def x_first(way, zrel, r):
            xrel = 2 if way == RIGHT else 1
            ref = loc(block_of(xrel, zrel), r)
            arrived(xb + (way * 4 + zrel) * 2 + r, ref)
            if r == way and zrel != 3:
                send(xf + way * 4 + zrel, ref, ref, xdev[way])

        def x_second(way, zrel):
            arrived(xf + way * 4 + zrel, loc(block_of(3, zrel), way))

        return z_own, x_direct, z_in, x_first, x_second

    w_z_own, w_x_direct, w_z_in, w_x_first, w_x_second = gather("w", wloc)

    wown[0] = share_of(0, c)
    wown[1] = share_of(1, c)

    def to_y(r):
        arrived(BASE["wsib"] + r, wsib.at[r])
        for yy in range(4):
            cols = slice(yy * 128, (yy + 1) * 128)
            wys[r, yy] = (wown[r, :, cols] + wsib[r, :, cols].astype(F32)).astype(BF16)
        for d in (1, 2, 3):
            send(BASE["wy"] + r * 3 + d - 1, wys.at[r, (y + d) % 4], wyr.at[r, d - 1], ydev[d])

    def own_w(r):
        total = wys[r, y].astype(F32)
        for d in (1, 2, 3):
            arrived(BASE["wy"] + r * 3 + d - 1, wyr.at[r, d - 1])
            total = total + wyr[r, d - 1].astype(F32)
        wg[rows_of(s, r), :] = total.astype(BF16)
        w_z_own(r)
        w_x_direct(0, r)

    to_y(0)
    to_y(1)
    for copy in small:
        copy.wait()
    q_load.wait()
    cot_load.wait()
    for h in range(8):
        cols = slice(h * 128, (h + 1) * 128)
        rows = slice((h % 4) * 16, (h % 4 + 1) * 16)
        wide = queries[:, cols].astype(F32)
        scale = lax.rsqrt(jnp.mean(wide * wide, axis=-1, keepdims=True) + epsilon)
        low = (wide * scale * qgain[...]).astype(BF16)
        qgb[h // 4, 0, :, rows, :] = low.reshape(16, 16, HD)
        gate = jnp.tanh(jnp.full((1, HD), hgate[h], F32))
        grad = (cot[:, cols].astype(F32) * gate).astype(BF16)
        qgb[h // 4, 1, :, rows, :] = grad.reshape(16, 16, HD)

    @pl.loop(0, 16)
    def _(i):
        first, last, seen = i * 0, i * 0, i * 0
        for b in range(16):
            hit = (block_image[b] == i).astype(jnp.int32)
            first = first + b * hit * (1 - seen)
            last = last + (b - last) * hit
            seen = seen + hit * (1 - seen)
        zero = jnp.zeros((64, HD), BF16)
        for part in range(2):
            for kind in range(2):
                qsend[i, part, kind, 0] = jnp.where(seen > 0, qgb[part, kind, first], zero)
                qsend[i, part, kind, 1] = jnp.where(last > first, qgb[part, kind, last], zero)

    place_z = g * 4 + z
    for step, dz in enumerate((2, -2, 1, -1, 0)):
        to_z = (place_z + dz + 8) % 8

        @pl.when(to_z // 4 == c)
        def _(step=step, dz=dz, to_z=to_z):
            for xrel in (3, 1, 2, 0):
                owner = (to_z % 4) * 4 + xs[xrel]
                for part in range(2):
                    place = BASE["route"] + (step * 4 + xrel) * 2 + part
                    src, dst = qsend.at[owner, part], qin.at[s]
                    if dz == 2:
                        src, dst = src.at[0], dst.at[0]
                    if dz == -2:
                        src, dst = src.at[1], dst.at[1]
                    if dz == 0 and xrel == 0:
                        @pl.when(c == part)
                        def _(part=part):
                            qin[s] = qsend[s, part]

                        @pl.when(c != part)
                        def _(place=place, src=src, dst=dst):
                            send(place, src, dst, sib)
                    else:
                        send(place, src, dst, (to_z // 4, owner, 2 * y + part))

    own_w(0)
    own_w(1)
    for r in (0, 1):
        w_z_in(1, r)
        w_z_in(2, r)

    img_load.wait()
    for part in range(4):
        rows = slice(part * 64, (part + 1) * 64)
        lead = img[rows, :VD].astype(F32)
        center = jnp.mean(lead, axis=-1, keepdims=True)
        spread = jnp.mean((lead - center) ** 2, axis=-1, keepdims=True)
        lead = (lead - center) * lax.rsqrt(spread + epsilon)
        for k in range(VD // 128):
            cols = slice(k * 128, (k + 1) * 128)
            img[rows, cols] = (lead[:, cols] * ngain[k:k + 1, :]).astype(BF16)

    for r in (0, 1):
        w_x_first(RIGHT, 0, r)
        w_x_first(LEFT, 0, r)
    for r in (0, 1):
        w_z_in(3, r)
    for zrel in (1, 2, 3):
        for r in (0, 1):
            w_x_first(RIGHT, zrel, r)
            w_x_first(LEFT, zrel, r)
    for zrel in range(4):
        w_x_second(RIGHT, zrel)
        w_x_second(LEFT, zrel)
        cols = pl.ds(pl.multiple_of(zs[zrel] * (4 * WROWS), 128), 4 * WROWS)
        product = jnp.dot(img[:, cols], wg[cols, :], preferred_element_type=F32)
        if zrel == 0:
            projf[...] = product
        else:
            projf[...] += product

    made = projf[...]
    key_scale = lax.rsqrt(jnp.mean(made * made, axis=-1, keepdims=True) + epsilon)
    kvb[c] = jnp.where(c == 0, made * key_scale * kgain[...], made).astype(BF16)

    send(BASE["share"], kvb.at[c], kvb.at[c], sib)

    for step, dz in enumerate((2, -2, 1, -1, 0)):
        from_z = (z + 8 - dz) % 4
        for xrel in range(4):
            text = from_z * 4 + (x + (0, 3, 1, 2)[xrel]) % 4
            place = BASE["route"] + (step * 4 + xrel) * 2 + c
            dst = qin.at[text]
            if dz == 2:
                dst = dst.at[0]
            if dz == -2:
                dst = dst.at[1]
            if dz == 0 and xrel == 0:
                @pl.when(c != g)
                def _(place=place, dst=dst):
                    arrived(place, dst)
            else:
                arrived(place, dst)
    arrived(BASE["share"], kvb.at[other])

    gmade[...] = jnp.zeros((2, ROWS, HD), F32)

    @pl.loop(0, 8)
    def _(step):
        zz = (z + step // 2) % 4
        devices = [zz * 4 + (step % 2) * 2 + k for k in range(2)]
        low = jnp.concatenate([qin[t, 0].reshape(128, HD) for t in devices], axis=0)
        grad = jnp.concatenate([qin[t, 1].reshape(128, HD) for t in devices], axis=0)
        keys, values = kvb[0], kvb[1]
        scores = nt(keys, low) * INV
        usable = lax.broadcasted_iota(jnp.int32, (ROWS, ROWS), 0) < image_len[s]
        raised = jnp.where(usable, jnp.exp(scores), 0.0)
        weights = raised / jnp.sum(raised, axis=0, keepdims=True)
        weight_grads = nt(values, grad)
        inner = jnp.sum(weights * weight_grads, axis=0, keepdims=True)
        score_grads = (weights * (weight_grads - inner) * INV).astype(BF16)
        gmade[0] += jnp.dot(score_grads, low, preferred_element_type=F32)
        gmade[1] += jnp.dot(weights.astype(BF16), grad, preferred_element_type=F32)
        back = tn(score_grads, keys).astype(BF16)
        for k, t in enumerate(devices):
            dqout[t] = back[k * 128:(k + 1) * 128].reshape(2, 64, HD)

            place = BASE["back"] + ((16 + t - s) % 16) * 2 + c
            here = (g == 1) & (c == 1) & (t == s)

            @pl.when(here)
            def _(t=t):
                dqin[s, 1] = dqout[t]

            @pl.when(jnp.logical_not(here))
            def _(t=t, place=place):
                send(place, dqout.at[t], dqin.at[s, c], (1, t, 2 * y + g))

    send(BASE["gsib"], gmade.at[other], gsib, sib)
    arrived(BASE["gsib"], gsib)

    def half(r):
        return slice(r * HALF, (r + 1) * HALF)

    for r in (0, 1):
        total = gmade[c, half(r)] + gsib[half(r)]
        raw = projf[half(r)]
        scale = lax.rsqrt(jnp.mean(raw * raw, axis=-1, keepdims=True) + epsilon)
        scaled = total * kgain[...]
        back = scale * (
            scaled - raw * (scale * scale) * jnp.mean(scaled * raw, axis=-1, keepdims=True)
        )
        pgbuf[g, c, y, half(r)] = jnp.where(c == 0, back, total).astype(BF16)

    @pl.when(g == 1)
    def _():
        copy = send(BASE["pgx"], pgbuf.at[1, c, y], pgbuf.at[1, c, y], across)
        for image in range(16):
            for part in range(2):
                place = BASE["back"] + ((16 + s - image) % 16) * 2 + part
                if part == 0:
                    arrived(place, dqin.at[image, part])
                else:
                    @pl.when((c == 0) | (s != image))
                    def _(place=place, image=image):
                        arrived(place, dqin.at[image, 1])

        @pl.loop(0, 16)
        def _(b):
            mine = block_image[b]
            slot = b * 0
            for bb in range(16):
                hit = ((bb < b) & (block_image[bb] == mine)).astype(jnp.int32)
                slot = slot + hit * (1 - slot)
            for part in range(2):
                dqs[part, b] = dqin[mine, part, slot]

        for h in range(8):
            cols = slice(h * 128, (h + 1) * 128)
            rows = slice((h % 4) * 16, (h % 4 + 1) * 16)
            d = dqs[h // 4, :, rows, :].reshape(ROWS, HD).astype(F32) * qgain[...]
            wide = queries[:, cols].astype(F32)
            scale = lax.rsqrt(jnp.mean(wide * wide, axis=-1, keepdims=True) + epsilon)
            res = scale * (d - wide * (scale * scale) * jnp.mean(d * wide, axis=-1, keepdims=True))
            out[0, :, cols] = res.astype(BF16)
        copy.wait_send()

    @pl.when(g == 0)
    def _():
        mine = []
        for par in range(2):
            if par == 1:
                arrived(BASE["pgx"], pgbuf.at[1, c, y])
            own = pgbuf.at[par, c, y]
            for d in (2, 1, 3):
                mine.append(send(BASE["pgy"] + par * 3 + d - 1, own, own, ydev[d]))
            mine.append(send(BASE["pgs"] + par * 4, own, own, sib))
            for d in (1, 3, 2):
                ref = pgbuf.at[par, c, (y + 4 - d) % 4]
                arrived(BASE["pgy"] + par * 3 + d - 1, ref)
                mine.append(send(BASE["pgs"] + par * 4 + d, ref, ref, sib))
            if par == 1:
                for copy in kv_rest:
                    copy.wait()

            def term(kind):
                cat = jnp.concatenate([pgbuf[par, kind, yy] for yy in range(4)], axis=1)
                return nt(cat, kvall[par, kind])

            if par == 0:
                acc[...] = term(c)
            else:
                acc[...] += term(c)
            for d in (0, 1, 3, 2):
                arrived(BASE["pgs"] + par * 4 + d, pgbuf.at[par, other, (y + 4 - d) % 4])
            if par == 0:
                acc[...] += term(other)
            else:
                out[0] = (acc[...] + term(other)).astype(BF16)
        for copy in mine:
            copy.wait_send()

    for name, piece in (
        ("wsib", wsend.at[0]),
        ("wy", wys.at[0, 0]),
        ("wz", wg.at[0:WHALF, :]),
        ("wx", wg.at[0:WHALF, :]),
        ("wxf", wg.at[0:WHALF, :]),
        ("share", kvb.at[0]),
        ("gsib", gsib),
    ):
        for k in range(_sizes[name]):
            left(BASE[name] + k, piece)

    for step, dz in enumerate((2, -2, 1, -1, 0)):
        to_z = (place_z + dz + 8) % 8

        @pl.when(to_z // 4 == c)
        def _(step=step, dz=dz):
            piece = qsend.at[0, 0, 0] if abs(dz) == 2 else qsend.at[0, 0]
            for xrel in range(4):
                for part in range(2):
                    place = BASE["route"] + (step * 4 + xrel) * 2 + part
                    if dz == 0 and xrel == 0:
                        @pl.when(c != part)
                        def _(place=place):
                            left(place, piece)
                    else:
                        left(place, piece)

    for far in range(16):
        if far == 0:
            @pl.when((g == 0) | (c == 0))
            def _():
                left(BASE["back"] + c, dqout.at[0])
        else:
            left(BASE["back"] + far * 2 + c, dqout.at[0])


def per_device(
    image_states, norm_gain, proj_weight, kv_weight, key_gain, queries, query_gain, head_gate,
    cotangent, block_image, image_len,
):
    anywhere = pl.BlockSpec(memory_space=pl.ANY)
    vmem = pl.BlockSpec(memory_space=pltpu.VMEM)
    V = pltpu.VMEM
    scratch = [
        V((VD // 128, 128), F32),
        V((1, HD), F32),
        V((1, HD), F32),
        pltpu.SMEM((8,), F32),
        pltpu.SMEM((16,), jnp.int32),
        pltpu.SMEM((16,), jnp.int32),
        V((ROWS, VIN), BF16),
        V((WROWS, 1024), BF16),
        V((2, 2, 1024, 512), BF16),
        V((ROWS, 1024), BF16),
        V((ROWS, 1024), BF16),
        V((2, WHALF, 512), BF16),
        V((2, WHALF, 512), F32),
        V((2, WHALF, 512), BF16),
        V((2, 4, WHALF, HD), BF16),
        V((2, 3, WHALF, HD), BF16),
        V((VIN, HD), BF16),
        V((ROWS, HD), F32),
        V((2, ROWS, HD), BF16),
        V((2, 2, 16, 64, HD), BF16),
        V((16, 2, 2, 2, 64, HD), BF16),
        V((16, 2, 2, 64, HD), BF16),
        V((16, 2, 64, HD), BF16),
        V((16, 2, 2, 64, HD), BF16),
        V((2, 16, 64, HD), BF16),
        V((2, ROWS, HD), F32),
        V((ROWS, HD), F32),
        V((2, 2, 4, ROWS, HD), BF16),
        V((ROWS, 1024), F32),
        pltpu.SemaphoreType.DMA((PLACES,)),
        pltpu.SemaphoreType.DMA((PLACES,)),
        pltpu.SemaphoreType.DMA((32,)),
    ]
    return pl.pallas_call(
        kernel,
        out_shape=jax.ShapeDtypeStruct((1, ROWS, 1024), BF16),
        in_specs=[anywhere] * 11,
        out_specs=vmem,
        scratch_shapes=scratch,
        compiler_params=pltpu.CompilerParams(
            collective_id=0, has_side_effects=True, vmem_limit_bytes=60 * 2**20
        ),
    )(
        image_states.reshape(ROWS, VIN), norm_gain.reshape(VD // 128, 128), proj_weight, kv_weight,
        key_gain.reshape(1, HD), queries, query_gain.reshape(1, HD), head_gate, cotangent,
        block_image.reshape(16), image_len,
    )


def solution(mesh):
    placed = (
        P("seq", None, None), P(), P("seq", "mp"), P("mp", None), P(), P("seq", "mp"), P(),
        P("mp"), P("seq", "mp"), P("seq", None), P(),
    )
    return jax.shard_map(
        per_device, mesh=mesh, in_specs=placed, out_specs=P("group", "seq", "mp"), check_vma=False
    )
```

time: 115 us -> 79.3 us (0.69); the launches traced: 113 us -> 79.2 us
  Pallas kernels: 105 us -> 77.3 us
  local copies, waits for them, and re-layouts: 8.13 us -> 1.87 us
    pallas_call x1, Pallas kernels: 105 us -> 77.3 us  [per_device(): pl.pallas_call(kernel, out_shape=jax.ShapeDtypeStruct((1, ROWS, 1024), BF...]
    unnamed x16 -> x1, local copies, waits for them, and re-layouts: 7.43 us -> 1.87 us
where the time goes in v3:
time: 79.3 us; the launch traced here: 79.2 us
  Pallas kernels  77.3 us (97%)
  local copies, waits for them, and re-layouts  1.87 us (2%)
    pallas_call x1, Pallas kernels, per_device(): pl.pallas_call(kernel, out_shape=jax.ShapeDtypeStruct((1, ROWS, 1024), BF...  77.3 us
    unnamed x1, local copies, waits for them, and re-layouts  1.87 us

profile of v3, /device:TPU:1, one launch (start us, length us, event | category | flops | bytes accessed | tf_op | source)
XLA Modules:
  0.0 79.2 jit_solution(5407610105730235599)
XLA Ops:
  0.0 77.3 %shard_map.109 = bf16[1,256,1024]{2,1,0:T(8,128)(2,1)} custom-call(bf16[256,7680]{1,0:T(8,128)(2,1)} %bitcast.5, f32[10,128]{1,0:T(8,128)} %bitcast.6, bf16[480,1024]{1,0:T(8,128)(2,1)} %proj_hbm.1, bf16[1024,2048]{1,0:T(8,128)(2,1)} %kv_hbm.1, f32[1,128]{1,0:T(1,128)} %bitcast.7, bf16[256,1024]{1,0:T(8,128)(2,1)} %q_hbm.1, f32[1,128]{1,0:T(1,128)} %bitcast.8, ...), custom_call_target="tpu_custom_call" | custom-call | tf_op jit(solution)/shard_map/pallas_call | solution.py:543
  77.3 1.9 %copy.13 = bf16[1,256,1024]{2,1,0:T(8,128)(2,1)} copy(bf16[1,256,1024]{2,1,0:T(8,128)(2,1)} %shard_map.109) | data formatting | bytes 1048576

commit v4 on v3

--- a/solution.py
+++ b/solution.py
@@ -53,7 +53,7 @@
     ngain, kgain, qgain, hgate, block_image, image_len,
     img, proj, kvall, queries, cot,
     wsend, wown, wsib, wys, wyr, wg,
-    projf, kvb, qgb, qsend, qin, dqout, dqin, dqs,
+    projf, kvb, qsend, qin, dqout, dqin, dqs,
     gmade, gsib,
     pgbuf, acc,
     ssem, rsem, lsem,
@@ -93,6 +93,16 @@
     def arrived(place, dst):
         rc(place, dst, dst, sib).wait_recv()
 
+    barrier = pltpu.get_barrier_semaphore()
+    for dev in ydev[1:]:
+        pl.semaphore_signal(barrier, inc=1, device_id=dev, device_id_type=MESH)
+
+    @pl.loop(1, 64)
+    def _(k):
+        at = (g * 32 + s * 2 + c + k) % 64
+        dev = (at // 32, (at // 2) % 16, 2 * y + at % 2)
+        pl.semaphore_signal(barrier, inc=1, device_id=dev, device_id_type=MESH)
+
     local = {}
 
     def load(name, src, dst):
@@ -107,20 +117,6 @@
             kvall.at[par, kind, :, yy * 128:(yy + 1) * 128],
         )
 
-    proj_load = load("proj", proj_hbm, proj)
-    proj_load.start()
-    kv_sib = [strip(g, other, yy) for yy in range(4)]
-    for copy in kv_sib:
-        copy.start()
-    kv_own = [strip(g, c, yy) for yy in range(4)]
-    for copy in kv_own:
-        copy.start()
-    q_load = load("q", q_hbm, queries)
-    q_load.start()
-    cot_load = load("cot", cot_hbm, cot)
-    cot_load.start()
-    img_load = load("img", img_hbm, img)
-    img_load.start()
     small = [
         load("ngain", ngain_hbm, ngain),
         load("kgain", kgain_hbm, kgain),
@@ -131,6 +127,20 @@
     ]
     for copy in small:
         copy.start()
+    q_load = load("q", q_hbm, queries)
+    q_load.start()
+    cot_load = load("cot", cot_hbm, cot)
+    cot_load.start()
+    proj_load = load("proj", proj_hbm, proj)
+    proj_load.start()
+    kv_sib = [strip(g, other, yy) for yy in range(4)]
+    for copy in kv_sib:
+        copy.start()
+    kv_own = [strip(g, c, yy) for yy in range(4)]
+    for copy in kv_own:
+        copy.start()
+    img_load = load("img", img_hbm, img)
+    img_load.start()
     kv_rest = [strip(1 - g, kind, yy) for kind in range(2) for yy in range(4)]
 
     @pl.when(g == 0)
@@ -138,112 +148,11 @@
         for copy in kv_rest:
             copy.start()
 
-    barrier = pltpu.get_barrier_semaphore()
-    for dev in ydev[1:]:
-        pl.semaphore_signal(barrier, inc=1, device_id=dev, device_id_type=MESH)
-
-    @pl.loop(1, 64)
-    def _(k):
-        at = (g * 32 + s * 2 + c + k) % 64
-        dev = (at // 32, (at // 2) % 16, 2 * y + at % 2)
-        pl.semaphore_signal(barrier, inc=1, device_id=dev, device_id_type=MESH)
-
-    proj_load.wait()
-    for copy in kv_sib:
-        copy.wait()
-
-    def share_of(r, kind):
-        return jnp.dot(
-            proj[r * WHALF:(r + 1) * WHALF, :], kvall[g, kind], preferred_element_type=F32
-        )
-
-    wsend[0] = share_of(0, other).astype(BF16)
-    pl.semaphore_wait(barrier, 66)
-    send(BASE["wsib"], wsend.at[0], wsib.at[0], sib)
-    wsend[1] = share_of(1, other).astype(BF16)
-    send(BASE["wsib"] + 1, wsend.at[1], wsib.at[1], sib)
-    for copy in kv_own:
-        copy.wait()
-
-    def rows_of(block, r):
-        return pl.ds(pl.multiple_of(block * WROWS + r * WHALF, 16), WHALF)
-
-    def wloc(block, r):
-        return wg.at[rows_of(block, r), :]
-
-    def block_of(xrel, zrel):
-        return zs[zrel] * 4 + xs[xrel]
-
-    def gather(kind, loc):
-        zb, xb, xf = BASE[kind + "z"], BASE[kind + "x"], BASE[kind + "xf"]
-
-        def z_own(r):
-            ref = loc(block_of(0, 0), r)
-            for k in (1, 2, 3):
-                send(zb + (k - 1) * 2 + r, ref, ref, zdev[k - 1])
-
-        def x_direct(zrel, r):
-            ref = loc(block_of(0, zrel), r)
-            for way in (RIGHT, LEFT):
-                send(xb + (way * 4 + zrel) * 2 + r, ref, ref, xdev[way])
-            if zrel == 3:
-                send(xf + r * 4 + zrel, ref, ref, xfar)
-
-        def z_in(zrel, r):
-            k = (0, 2, 1, 3)[zrel]
-            arrived(zb + (k - 1) * 2 + r, loc(block_of(0, zrel), r))
-            x_direct(zrel, r)
-
-        def x_first(way, zrel, r):
-            xrel = 2 if way == RIGHT else 1
-            ref = loc(block_of(xrel, zrel), r)
-            arrived(xb + (way * 4 + zrel) * 2 + r, ref)
-            if r == way and zrel != 3:
-                send(xf + way * 4 + zrel, ref, ref, xdev[way])
-
-        def x_second(way, zrel):
-            arrived(xf + way * 4 + zrel, loc(block_of(3, zrel), way))
-
-        return z_own, x_direct, z_in, x_first, x_second
-
-    w_z_own, w_x_direct, w_z_in, w_x_first, w_x_second = gather("w", wloc)
-
-    wown[0] = share_of(0, c)
-    wown[1] = share_of(1, c)
-
-    def to_y(r):
-        arrived(BASE["wsib"] + r, wsib.at[r])
-        for yy in range(4):
-            cols = slice(yy * 128, (yy + 1) * 128)
-            wys[r, yy] = (wown[r, :, cols] + wsib[r, :, cols].astype(F32)).astype(BF16)
-        for d in (1, 2, 3):
-            send(BASE["wy"] + r * 3 + d - 1, wys.at[r, (y + d) % 4], wyr.at[r, d - 1], ydev[d])
-
-    def own_w(r):
-        total = wys[r, y].astype(F32)
-        for d in (1, 2, 3):
-            arrived(BASE["wy"] + r * 3 + d - 1, wyr.at[r, d - 1])
-            total = total + wyr[r, d - 1].astype(F32)
-        wg[rows_of(s, r), :] = total.astype(BF16)
-        w_z_own(r)
-        w_x_direct(0, r)
-
-    to_y(0)
-    to_y(1)
     for copy in small:
         copy.wait()
     q_load.wait()
     cot_load.wait()
-    for h in range(8):
-        cols = slice(h * 128, (h + 1) * 128)
-        rows = slice((h % 4) * 16, (h % 4 + 1) * 16)
-        wide = queries[:, cols].astype(F32)
-        scale = lax.rsqrt(jnp.mean(wide * wide, axis=-1, keepdims=True) + epsilon)
-        low = (wide * scale * qgain[...]).astype(BF16)
-        qgb[h // 4, 0, :, rows, :] = low.reshape(16, 16, HD)
-        gate = jnp.tanh(jnp.full((1, HD), hgate[h], F32))
-        grad = (cot[:, cols].astype(F32) * gate).astype(BF16)
-        qgb[h // 4, 1, :, rows, :] = grad.reshape(16, 16, HD)
+    gates = [jnp.tanh(jnp.full((1, HD), hgate[h], F32)) for h in range(8)]
 
     @pl.loop(0, 16)
     def _(i):
@@ -253,11 +162,16 @@
             first = first + b * hit * (1 - seen)
             last = last + (b - last) * hit
             seen = seen + hit * (1 - seen)
-        zero = jnp.zeros((64, HD), BF16)
-        for part in range(2):
-            for kind in range(2):
-                qsend[i, part, kind, 0] = jnp.where(seen > 0, qgb[part, kind, first], zero)
-                qsend[i, part, kind, 1] = jnp.where(last > first, qgb[part, kind, last], zero)
+        zero = jnp.zeros((16, HD), BF16)
+        for slot, (at, use) in enumerate(((first, seen > 0), (last, last > first))):
+            for h in range(8):
+                cols = slice(h * 128, (h + 1) * 128)
+                rows = slice((h % 4) * 16, (h % 4 + 1) * 16)
+                qsend[i, h // 4, 0, slot, rows, :] = jnp.where(use, queries[at, :, cols], zero)
+                grad = (cot[at, :, cols].astype(F32) * gates[h]).astype(BF16)
+                qsend[i, h // 4, 1, slot, rows, :] = jnp.where(use, grad, zero)
+
+    pl.semaphore_wait(barrier, 66)
 
     place_z = g * 4 + z
     for step, dz in enumerate((2, -2, 1, -1, 0)):
@@ -285,49 +199,94 @@
                     else:
                         send(place, src, dst, (to_z // 4, owner, 2 * y + part))
 
+    proj_load.wait()
+    for copy in kv_sib:
+        copy.wait()
+
+    def share_of(r, kind):
+        return jnp.dot(
+            proj[r * WHALF:(r + 1) * WHALF, :], kvall[g, kind], preferred_element_type=F32
+        )
+
+    wsend[0] = share_of(0, other).astype(BF16)
+    send(BASE["wsib"], wsend.at[0], wsib.at[0], sib)
+    wsend[1] = share_of(1, other).astype(BF16)
+    send(BASE["wsib"] + 1, wsend.at[1], wsib.at[1], sib)
+    for copy in kv_own:
+        copy.wait()
+
+    def rows_of(block, r):
+        return pl.ds(pl.multiple_of(block * WROWS + r * WHALF, 16), WHALF)
+
+    def wloc(block, r):
+        return wg.at[rows_of(block, r), :]
+
+    def block_of(xrel, zrel):
+        return zs[zrel] * 4 + xs[xrel]
+
+    def gather(kind, loc):
+        zb, xb, xf = BASE[kind + "z"], BASE[kind + "x"], BASE[kind + "xf"]
+
+        def z_own(r):
+            ref = loc(block_of(0, 0), r)
+            for k in (1, 2, 3):
+                send(zb + (k - 1) * 2 + r, ref, ref, zdev[k - 1])
+
+        def x_direct(zrel, r):
+            ref = loc(block_of(0, zrel), r)
+            for way in (RIGHT, LEFT):
+                send(xb + (way * 4 + zrel) * 2 + r, ref, ref, xdev[way])
+            if zrel == 3:
+                send(xf + r * 4 + zrel, ref, ref, xfar)
+
+        def z_in(zrel, r):
+            k = (0, 2, 1, 3)[zrel]
+            arrived(zb + (k - 1) * 2 + r, loc(block_of(0, zrel), r))
+            x_direct(zrel, r)
+
+        def x_first(way, zrel, r):
+            xrel = 2 if way == RIGHT else 1
+            ref = loc(block_of(xrel, zrel), r)
+            arrived(xb + (way * 4 + zrel) * 2 + r, ref)
+            if r == way and zrel != 3:
+                send(xf + way * 4 + zrel, ref, ref, xdev[way])
+
+        def x_second(way, zrel):
+            arrived(xf + way * 4 + zrel, loc(block_of(3, zrel), way))
+
+        return z_own, x_direct, z_in, x_first, x_second
+
+    w_z_own, w_x_direct, w_z_in, w_x_first, w_x_second = gather("w", wloc)
+
+    wown[0] = share_of(0, c)
+    wown[1] = share_of(1, c)
+
+    def to_y(r):
+        arrived(BASE["wsib"] + r, wsib.at[r])
+        for yy in range(4):
+            cols = slice(yy * 128, (yy + 1) * 128)
+            wys[r, yy] = (wown[r, :, cols] + wsib[r, :, cols].astype(F32)).astype(BF16)
+        for d in (1, 2, 3):
+            send(BASE["wy"] + r * 3 + d - 1, wys.at[r, (y + d) % 4], wyr.at[r, d - 1], ydev[d])
+
+    def own_w(r):
+        total = wys[r, y].astype(F32)
+        for d in (1, 2, 3):
+            arrived(BASE["wy"] + r * 3 + d - 1, wyr.at[r, d - 1])
+            total = total + wyr[r, d - 1].astype(F32)
+        wg[rows_of(s, r), :] = total.astype(BF16)
+        w_z_own(r)
+        w_x_direct(0, r)
+
+    to_y(0)
+    to_y(1)
     own_w(0)
     own_w(1)
     for r in (0, 1):
         w_z_in(1, r)
         w_z_in(2, r)
 
-    img_load.wait()
-    for part in range(4):
-        rows = slice(part * 64, (part + 1) * 64)
-        lead = img[rows, :VD].astype(F32)
-        center = jnp.mean(lead, axis=-1, keepdims=True)
-        spread = jnp.mean((lead - center) ** 2, axis=-1, keepdims=True)
-        lead = (lead - center) * lax.rsqrt(spread + epsilon)
-        for k in range(VD // 128):
-            cols = slice(k * 128, (k + 1) * 128)
-            img[rows, cols] = (lead[:, cols] * ngain[k:k + 1, :]).astype(BF16)
-
-    for r in (0, 1):
-        w_x_first(RIGHT, 0, r)
-        w_x_first(LEFT, 0, r)
-    for r in (0, 1):
-        w_z_in(3, r)
-    for zrel in (1, 2, 3):
-        for r in (0, 1):
-            w_x_first(RIGHT, zrel, r)
-            w_x_first(LEFT, zrel, r)
-    for zrel in range(4):
-        w_x_second(RIGHT, zrel)
-        w_x_second(LEFT, zrel)
-        cols = pl.ds(pl.multiple_of(zs[zrel] * (4 * WROWS), 128), 4 * WROWS)
-        product = jnp.dot(img[:, cols], wg[cols, :], preferred_element_type=F32)
-        if zrel == 0:
-            projf[...] = product
-        else:
-            projf[...] += product
-
-    made = projf[...]
-    key_scale = lax.rsqrt(jnp.mean(made * made, axis=-1, keepdims=True) + epsilon)
-    kvb[c] = jnp.where(c == 0, made * key_scale * kgain[...], made).astype(BF16)
-
-    send(BASE["share"], kvb.at[c], kvb.at[c], sib)
-
-    for step, dz in enumerate((2, -2, 1, -1, 0)):
+    def route_in(step, dz):
         from_z = (z + 8 - dz) % 4
         for xrel in range(4):
             text = from_z * 4 + (x + (0, 3, 1, 2)[xrel]) % 4
@@ -343,11 +302,67 @@
                     arrived(place, dst)
             else:
                 arrived(place, dst)
+            if dz != -2:
+                wide = qin[text, 0].reshape(128, HD).astype(F32)
+                scale = lax.rsqrt(jnp.mean(wide * wide, axis=-1, keepdims=True) + epsilon)
+                qin[text, 0] = (wide * scale * qgain[...]).astype(BF16).reshape(2, 64, HD)
+
+    img_load.wait()
+    for part in range(4):
+        rows = slice(part * 64, (part + 1) * 64)
+        lead = img[rows, :VD].astype(F32)
+        center = jnp.mean(lead, axis=-1, keepdims=True)
+        spread = jnp.mean((lead - center) ** 2, axis=-1, keepdims=True)
+        lead = (lead - center) * lax.rsqrt(spread + epsilon)
+        for k in range(VD // 128):
+            cols = slice(k * 128, (k + 1) * 128)
+            img[rows, cols] = (lead[:, cols] * ngain[k:k + 1, :]).astype(BF16)
+
+    for r in (0, 1):
+        w_x_first(RIGHT, 0, r)
+        w_x_first(LEFT, 0, r)
+    for r in (0, 1):
+        w_z_in(3, r)
+    route_in(0, 2)
+    route_in(1, -2)
+    for zrel in (1, 2, 3):
+        for r in (0, 1):
+            w_x_first(RIGHT, zrel, r)
+            w_x_first(LEFT, zrel, r)
+        route_in(zrel + 1, (1, -1, 0)[zrel - 1])
+    for zrel in range(4):
+        w_x_second(RIGHT, zrel)
+        w_x_second(LEFT, zrel)
+        cols = pl.ds(pl.multiple_of(zs[zrel] * (4 * WROWS), 128), 4 * WROWS)
+        product = jnp.dot(img[:, cols], wg[cols, :], preferred_element_type=F32)
+        if zrel == 0:
+            projf[...] = product
+        else:
+            projf[...] += product
+
+    made = projf[...]
+    key_scale = lax.rsqrt(jnp.mean(made * made, axis=-1, keepdims=True) + epsilon)
+    kvb[c] = jnp.where(c == 0, made * key_scale * kgain[...], made).astype(BF16)
+
+    send(BASE["share"], kvb.at[c], kvb.at[c], sib)
+
     arrived(BASE["share"], kvb.at[other])
 
+    def give_back(t):
+        here = (g == 1) & (c == 1) & (t == s)
+
+        @pl.when(here)
+        def _():
+            dqin[s, 1] = dqout[t]
+
+        @pl.when(jnp.logical_not(here))
+        def _():
+            place = BASE["back"] + ((16 + t - s) % 16) * 2 + c
+            send(place, dqout.at[t], dqin.at[s, c], (1, t, 2 * y + g))
+
     gmade[...] = jnp.zeros((2, ROWS, HD), F32)
 
-    @pl.loop(0, 8)
+    @pl.loop(0, 8, unroll=2)
     def _(step):
         zz = (z + step // 2) % 4
         devices = [zz * 4 + (step % 2) * 2 + k for k in range(2)]
@@ -357,28 +372,23 @@
         scores = nt(keys, low) * INV
         usable = lax.broadcasted_iota(jnp.int32, (ROWS, ROWS), 0) < image_len[s]
         raised = jnp.where(usable, jnp.exp(scores), 0.0)
-        weights = raised / jnp.sum(raised, axis=0, keepdims=True)
+        over = 1.0 / jnp.sum(raised, axis=0, keepdims=True)
         weight_grads = nt(values, grad)
-        inner = jnp.sum(weights * weight_grads, axis=0, keepdims=True)
-        score_grads = (weights * (weight_grads - inner) * INV).astype(BF16)
+        inner = jnp.sum(raised * weight_grads, axis=0, keepdims=True) * over
+        score_grads = (raised * (over * INV) * (weight_grads - inner)).astype(BF16)
         gmade[0] += jnp.dot(score_grads, low, preferred_element_type=F32)
-        gmade[1] += jnp.dot(weights.astype(BF16), grad, preferred_element_type=F32)
+        gmade[1] += jnp.dot((raised * over).astype(BF16), grad, preferred_element_type=F32)
         back = tn(score_grads, keys).astype(BF16)
         for k, t in enumerate(devices):
             dqout[t] = back[k * 128:(k + 1) * 128].reshape(2, 64, HD)
 
-            place = BASE["back"] + ((16 + t - s) % 16) * 2 + c
-            here = (g == 1) & (c == 1) & (t == s)
-
-            @pl.when(here)
+
+            @pl.when(g == 0)
             def _(t=t):
-                dqin[s, 1] = dqout[t]
-
-            @pl.when(jnp.logical_not(here))
-            def _(t=t, place=place):
-                send(place, dqout.at[t], dqin.at[s, c], (1, t, 2 * y + g))
+                give_back(t)
 
     send(BASE["gsib"], gmade.at[other], gsib, sib)
+
     arrived(BASE["gsib"], gsib)
 
     def half(r):
@@ -397,6 +407,11 @@
     @pl.when(g == 1)
     def _():
         copy = send(BASE["pgx"], pgbuf.at[1, c, y], pgbuf.at[1, c, y], across)
+
+        @pl.loop(0, 16)
+        def _(far):
+            give_back((s + far) % 16)
+
         for image in range(16):
             for part in range(2):
                 place = BASE["back"] + ((16 + s - image) % 16) * 2 + part
@@ -421,7 +436,7 @@
             cols = slice(h * 128, (h + 1) * 128)
             rows = slice((h % 4) * 16, (h % 4 + 1) * 16)
             d = dqs[h // 4, :, rows, :].reshape(ROWS, HD).astype(F32) * qgain[...]
-            wide = queries[:, cols].astype(F32)
+            wide = queries[:, :, cols].reshape(ROWS, HD).astype(F32)
             scale = lax.rsqrt(jnp.mean(wide * wide, axis=-1, keepdims=True) + epsilon)
             res = scale * (d - wide * (scale * scale) * jnp.mean(d * wide, axis=-1, keepdims=True))
             out[0, :, cols] = res.astype(BF16)
@@ -516,8 +531,8 @@
         V((ROWS, VIN), BF16),
         V((WROWS, 1024), BF16),
         V((2, 2, 1024, 512), BF16),
-        V((ROWS, 1024), BF16),
-        V((ROWS, 1024), BF16),
+        V((16, 16, 1024), BF16),
+        V((16, 16, 1024), BF16),
         V((2, WHALF, 512), BF16),
         V((2, WHALF, 512), F32),
         V((2, WHALF, 512), BF16),
@@ -526,7 +541,6 @@
         V((VIN, HD), BF16),
         V((ROWS, HD), F32),
         V((2, ROWS, HD), BF16),
-        V((2, 2, 16, 64, HD), BF16),
         V((16, 2, 2, 2, 64, HD), BF16),
         V((16, 2, 2, 64, HD), BF16),
         V((16, 2, 64, HD), BF16),
@@ -551,7 +565,8 @@
         ),
     )(
         image_states.reshape(ROWS, VIN), norm_gain.reshape(VD // 128, 128), proj_weight, kv_weight,
-        key_gain.reshape(1, HD), queries, query_gain.reshape(1, HD), head_gate, cotangent,
+        key_gain.reshape(1, HD), queries.reshape(16, 16, 1024), query_gain.reshape(1, HD),
+        head_gate, cotangent.reshape(16, 16, 1024),
         block_image.reshape(16), image_len,
     )
 

time: 79.3 us -> 76 us (0.958)
  Pallas kernels: 77.3 us -> 74 us
    pallas_call x1, Pallas kernels: 77.3 us -> 74 us  [per_device(): pl.pallas_call(kernel, out_shape=jax.ShapeDtypeStruct((1, ROWS, 1024), BF...]
where the time goes in v4:
time: 76 us; the launch traced here: 75.9 us
  Pallas kernels  74 us (97%)
  local copies, waits for them, and re-layouts  1.87 us (2%)
    pallas_call x1, Pallas kernels, per_device(): pl.pallas_call(kernel, out_shape=jax.ShapeDtypeStruct((1, ROWS, 1024), BF...  74 us
    unnamed x1, local copies, waits for them, and re-layouts  1.87 us

profile of v4, /device:TPU:1, one launch (start us, length us, event | category | flops | bytes accessed | tf_op | source)
XLA Modules:
  0.0 75.9 jit_solution(7160587680157770747)
XLA Ops:
  0.0 74.0 %shard_map.109 = bf16[1,256,1024]{2,1,0:T(8,128)(2,1)} custom-call(bf16[256,7680]{1,0:T(8,128)(2,1)} %bitcast.7, f32[10,128]{1,0:T(8,128)} %bitcast.10, bf16[480,1024]{1,0:T(8,128)(2,1)} %proj_hbm.1, bf16[1024,2048]{1,0:T(8,128)(2,1)} %kv_hbm.1, f32[1,128]{1,0:T(1,128)} %bitcast.11, bf16[16,16,1024]{2,1,0:T(8,128)(2,1)} %bitcast.8, f32[1,128]{1,0:T(1,128)} %bitcast.12, ...), custom_call_target="tpu_custom_call" | custom-call | tf_op jit(solution)/shard_map/pallas_call | solution.py:557
  74.0 1.9 %copy.13 = bf16[1,256,1024]{2,1,0:T(8,128)(2,1)} copy(bf16[1,256,1024]{2,1,0:T(8,128)(2,1)} %shard_map.109) | data formatting | bytes 1048576

commit v5 on v4

--- a/solution.py
+++ b/solution.py
@@ -21,7 +21,7 @@
 RIGHT, LEFT = 0, 1
 
 _sizes = dict(
-    wsib=2, wy=6, route=40,
+    wsib=4, wy=12, route=40,
     wz=6, wx=16, wxf=8,
     share=1, gsib=1,
     pgx=1, pgy=6, pgs=8, back=32,
@@ -52,7 +52,7 @@
     out,
     ngain, kgain, qgain, hgate, block_image, image_len,
     img, proj, kvall, queries, cot,
-    wsend, wown, wsib, wys, wyr, wg,
+    wsend, wsib, wys, wyr, wg,
     projf, kvb, qsend, qin, dqout, dqin, dqs,
     gmade, gsib,
     pgbuf, acc,
@@ -140,13 +140,7 @@
     for copy in kv_own:
         copy.start()
     img_load = load("img", img_hbm, img)
-    img_load.start()
     kv_rest = [strip(1 - g, kind, yy) for kind in range(2) for yy in range(4)]
-
-    @pl.when(g == 0)
-    def _():
-        for copy in kv_rest:
-            copy.start()
 
     for copy in small:
         copy.wait()
@@ -154,7 +148,7 @@
     cot_load.wait()
     gates = [jnp.tanh(jnp.full((1, HD), hgate[h], F32)) for h in range(8)]
 
-    @pl.loop(0, 16)
+    @pl.loop(0, 16, unroll=4)
     def _(i):
         first, last, seen = i * 0, i * 0, i * 0
         for b in range(16):
@@ -174,45 +168,39 @@
     pl.semaphore_wait(barrier, 66)
 
     place_z = g * 4 + z
-    for step, dz in enumerate((2, -2, 1, -1, 0)):
-        to_z = (place_z + dz + 8) % 8
-
-        @pl.when(to_z // 4 == c)
-        def _(step=step, dz=dz, to_z=to_z):
-            for xrel in (3, 1, 2, 0):
-                owner = (to_z % 4) * 4 + xs[xrel]
-                for part in range(2):
-                    place = BASE["route"] + (step * 4 + xrel) * 2 + part
-                    src, dst = qsend.at[owner, part], qin.at[s]
-                    if dz == 2:
-                        src, dst = src.at[0], dst.at[0]
-                    if dz == -2:
-                        src, dst = src.at[1], dst.at[1]
-                    if dz == 0 and xrel == 0:
-                        @pl.when(c == part)
-                        def _(part=part):
-                            qin[s] = qsend[s, part]
-
-                        @pl.when(c != part)
-                        def _(place=place, src=src, dst=dst):
-                            send(place, src, dst, sib)
-                    else:
-                        send(place, src, dst, (to_z // 4, owner, 2 * y + part))
+
+    def route(which):
+        for step, dz in enumerate((2, -2, 1, -1, 0)):
+            if dz not in which:
+                continue
+            to_z = (place_z + dz + 8) % 8
+
+            @pl.when(to_z // 4 == c)
+            def _(step=step, dz=dz, to_z=to_z):
+                for xrel in (3, 1, 2, 0):
+                    owner = (to_z % 4) * 4 + xs[xrel]
+                    for part in range(2):
+                        place = BASE["route"] + (step * 4 + xrel) * 2 + part
+                        src, dst = qsend.at[owner, part], qin.at[s]
+                        if dz == 2:
+                            src, dst = src.at[0], dst.at[0]
+                        if dz == -2:
+                            src, dst = src.at[1], dst.at[1]
+                        if dz == 0 and xrel == 0:
+                            @pl.when(c == part)
+                            def _(part=part):
+                                qin[s] = qsend[s, part]
+
+                            @pl.when(c != part)
+                            def _(place=place, src=src, dst=dst):
+                                send(place, src, dst, sib)
+                        else:
+                            send(place, src, dst, (to_z // 4, owner, 2 * y + part))
+
+    route((1, -1, 0))
 
     proj_load.wait()
     for copy in kv_sib:
-        copy.wait()
-
-    def share_of(r, kind):
-        return jnp.dot(
-            proj[r * WHALF:(r + 1) * WHALF, :], kvall[g, kind], preferred_element_type=F32
-        )
-
-    wsend[0] = share_of(0, other).astype(BF16)
-    send(BASE["wsib"], wsend.at[0], wsib.at[0], sib)
-    wsend[1] = share_of(1, other).astype(BF16)
-    send(BASE["wsib"] + 1, wsend.at[1], wsib.at[1], sib)
-    for copy in kv_own:
         copy.wait()
 
     def rows_of(block, r):
@@ -236,8 +224,6 @@
             ref = loc(block_of(0, zrel), r)
             for way in (RIGHT, LEFT):
                 send(xb + (way * 4 + zrel) * 2 + r, ref, ref, xdev[way])
-            if zrel == 3:
-                send(xf + r * 4 + zrel, ref, ref, xfar)
 
         def z_in(zrel, r):
             k = (0, 2, 1, 3)[zrel]
@@ -248,7 +234,7 @@
             xrel = 2 if way == RIGHT else 1
             ref = loc(block_of(xrel, zrel), r)
             arrived(xb + (way * 4 + zrel) * 2 + r, ref)
-            if r == way and zrel != 3:
+            if r == way:
                 send(xf + way * 4 + zrel, ref, ref, xdev[way])
 
         def x_second(way, zrel):
@@ -258,30 +244,61 @@
 
     w_z_own, w_x_direct, w_z_in, w_x_first, w_x_second = gather("w", wloc)
 
-    wown[0] = share_of(0, c)
-    wown[1] = share_of(1, c)
-
-    def to_y(r):
-        arrived(BASE["wsib"] + r, wsib.at[r])
+    def part_of(q):
+        first, size = ((0, 128), (128, 112), (240, 128), (368, 112))[q]
+        return slice(first, first + size)
+
+    def share_of(q, kind):
+        return jnp.dot(proj[part_of(q), :], kvall[g, kind], preferred_element_type=F32)
+
+    def to_sib(q):
+        rows = part_of(q)
+        wsend[rows, :] = share_of(q, other).astype(BF16)
+        send(BASE["wsib"] + q, wsend.at[rows, :], wsib.at[rows, :], sib)
+
+    def to_y(q):
+        rows = part_of(q)
+        own = share_of(q, c)
+        arrived(BASE["wsib"] + q, wsib.at[rows, :])
         for yy in range(4):
             cols = slice(yy * 128, (yy + 1) * 128)
-            wys[r, yy] = (wown[r, :, cols] + wsib[r, :, cols].astype(F32)).astype(BF16)
-        for d in (1, 2, 3):
-            send(BASE["wy"] + r * 3 + d - 1, wys.at[r, (y + d) % 4], wyr.at[r, d - 1], ydev[d])
+            wys[yy, rows, :] = (own[:, cols] + wsib[rows, cols].astype(F32)).astype(BF16)
+        for d in (2, 1, 3):
+            send(
+                BASE["wy"] + q * 3 + d - 1,
+                wys.at[(y + d) % 4, rows, :],
+                wyr.at[d - 1, rows, :],
+                ydev[d],
+            )
 
     def own_w(r):
-        total = wys[r, y].astype(F32)
-        for d in (1, 2, 3):
-            arrived(BASE["wy"] + r * 3 + d - 1, wyr.at[r, d - 1])
-            total = total + wyr[r, d - 1].astype(F32)
-        wg[rows_of(s, r), :] = total.astype(BF16)
+        for q in (2 * r, 2 * r + 1):
+            rows = part_of(q)
+            total = wys[y, rows, :].astype(F32)
+            for d in (1, 2, 3):
+                arrived(BASE["wy"] + q * 3 + d - 1, wyr.at[d - 1, rows, :])
+                total = total + wyr[d - 1, rows, :].astype(F32)
+            start = pl.multiple_of(s * WROWS + rows.start, 16)
+            wg[pl.ds(start, rows.stop - rows.start), :] = total.astype(BF16)
         w_z_own(r)
         w_x_direct(0, r)
 
-    to_y(0)
-    to_y(1)
+    to_sib(0)
+    for copy in kv_own:
+        copy.wait()
+    for q in range(4):
+        if q < 3:
+            to_sib(q + 1)
+        to_y(q)
+    img_load.start()
+
+    @pl.when(g == 0)
+    def _():
+        for copy in kv_rest:
+            copy.start()
     own_w(0)
     own_w(1)
+    route((2, -2))
     for r in (0, 1):
         w_z_in(1, r)
         w_z_in(2, r)
@@ -323,8 +340,6 @@
         w_x_first(LEFT, 0, r)
     for r in (0, 1):
         w_z_in(3, r)
-    route_in(0, 2)
-    route_in(1, -2)
     for zrel in (1, 2, 3):
         for r in (0, 1):
             w_x_first(RIGHT, zrel, r)
@@ -362,10 +377,8 @@
 
     gmade[...] = jnp.zeros((2, ROWS, HD), F32)
 
-    @pl.loop(0, 8, unroll=2)
-    def _(step):
-        zz = (z + step // 2) % 4
-        devices = [zz * 4 + (step % 2) * 2 + k for k in range(2)]
+    def attend(zz, step):
+        devices = [zz * 4 + step * 2 + k for k in range(2)]
         low = jnp.concatenate([qin[t, 0].reshape(128, HD) for t in devices], axis=0)
         grad = jnp.concatenate([qin[t, 1].reshape(128, HD) for t in devices], axis=0)
         keys, values = kvb[0], kvb[1]
@@ -386,6 +399,17 @@
             @pl.when(g == 0)
             def _(t=t):
                 give_back(t)
+
+    for step in range(2):
+        attend((z + 0) % 4, step)
+    for step in range(2):
+        attend((z + 3) % 4, step)
+    for step in range(2):
+        attend((z + 1) % 4, step)
+    route_in(0, 2)
+    route_in(1, -2)
+    for step in range(2):
+        attend((z + 2) % 4, step)
 
     send(BASE["gsib"], gmade.at[other], gsib, sib)
 
@@ -478,8 +502,6 @@
             copy.wait_send()
 
     for name, piece in (
-        ("wsib", wsend.at[0]),
-        ("wy", wys.at[0, 0]),
         ("wz", wg.at[0:WHALF, :]),
         ("wx", wg.at[0:WHALF, :]),
         ("wxf", wg.at[0:WHALF, :]),
@@ -488,6 +510,11 @@
     ):
         for k in range(_sizes[name]):
             left(BASE[name] + k, piece)
+    for q in range(4):
+        rows = part_of(q)
+        left(BASE["wsib"] + q, wsend.at[rows, :])
+        for d in (1, 2, 3):
+            left(BASE["wy"] + q * 3 + d - 1, wys.at[0, rows, :])
 
     for step, dz in enumerate((2, -2, 1, -1, 0)):
         to_z = (place_z + dz + 8) % 8
@@ -533,11 +560,10 @@
         V((2, 2, 1024, 512), BF16),
         V((16, 16, 1024), BF16),
         V((16, 16, 1024), BF16),
-        V((2, WHALF, 512), BF16),
-        V((2, WHALF, 512), F32),
-        V((2, WHALF, 512), BF16),
-        V((2, 4, WHALF, HD), BF16),
-        V((2, 3, WHALF, HD), BF16),
+        V((WROWS, 512), BF16),
+        V((WROWS, 512), BF16),
+        V((4, WROWS, HD), BF16),
+        V((3, WROWS, HD), BF16),
         V((VIN, HD), BF16),
         V((ROWS, HD), F32),
         V((2, ROWS, HD), BF16),

time: 76 us -> 75 us (0.987); the launches traced: 75.9 us -> 74 us
  Pallas kernels: 74 us -> 72.1 us
    pallas_call x1, Pallas kernels: 74 us -> 72.1 us  [per_device(): pl.pallas_call(kernel, out_shape=jax.ShapeDtypeStruct((1, ROWS, 1024), BF...]
where the time goes in v5:
time: 75 us; the launch traced here: 74 us
  Pallas kernels  72.1 us (96%)
  local copies, waits for them, and re-layouts  1.87 us (2%)
    pallas_call x1, Pallas kernels, per_device(): pl.pallas_call(kernel, out_shape=jax.ShapeDtypeStruct((1, ROWS, 1024), BF...  72.1 us
    unnamed x1, local copies, waits for them, and re-layouts  1.87 us

profile of v5, /device:TPU:1, one launch (start us, length us, event | category | flops | bytes accessed | tf_op | source)
XLA Modules:
  0.0 74.0 jit_solution(1382596275068007873)
XLA Ops:
  0.0 72.1 %shard_map.109 = bf16[1,256,1024]{2,1,0:T(8,128)(2,1)} custom-call(bf16[256,7680]{1,0:T(8,128)(2,1)} %bitcast.7, f32[10,128]{1,0:T(8,128)} %bitcast.10, bf16[480,1024]{1,0:T(8,128)(2,1)} %proj_hbm.1, bf16[1024,2048]{1,0:T(8,128)(2,1)} %kv_hbm.1, f32[1,128]{1,0:T(1,128)} %bitcast.11, bf16[16,16,1024]{2,1,0:T(8,128)(2,1)} %bitcast.8, f32[1,128]{1,0:T(1,128)} %bitcast.12, ...), custom_call_target="tpu_custom_call" | custom-call | tf_op jit(solution)/shard_map/pallas_call | solution.py:583
  72.1 1.9 %copy.13 = bf16[1,256,1024]{2,1,0:T(8,128)(2,1)} copy(bf16[1,256,1024]{2,1,0:T(8,128)(2,1)} %shard_map.109) | data formatting | bytes 1048576

commit v6 on v5

--- a/solution.py
+++ b/solution.py
@@ -436,6 +436,11 @@
         def _(far):
             give_back((s + far) % 16)
 
+        for h in range(8):
+            wide = queries[:, :, h * 128:(h + 1) * 128].reshape(ROWS, HD).astype(F32)
+            scale = lax.rsqrt(jnp.mean(wide * wide, axis=-1, keepdims=True) + epsilon)
+            acc[:, h * 128:(h + 1) * 128] = jnp.broadcast_to(scale, (ROWS, HD))
+
         for image in range(16):
             for part in range(2):
                 place = BASE["back"] + ((16 + s - image) % 16) * 2 + part
@@ -461,7 +466,7 @@
             rows = slice((h % 4) * 16, (h % 4 + 1) * 16)
             d = dqs[h // 4, :, rows, :].reshape(ROWS, HD).astype(F32) * qgain[...]
             wide = queries[:, :, cols].reshape(ROWS, HD).astype(F32)
-            scale = lax.rsqrt(jnp.mean(wide * wide, axis=-1, keepdims=True) + epsilon)
+            scale = acc[:, cols]
             res = scale * (d - wide * (scale * scale) * jnp.mean(d * wide, axis=-1, keepdims=True))
             out[0, :, cols] = res.astype(BF16)
         copy.wait_send()

time: 75 us -> 74.8 us (level)
  no operation moved by 1% of the time
where the time goes in v6:
time: 74.8 us; the launch traced here: 74 us
  Pallas kernels  72.1 us (96%)
  local copies, waits for them, and re-layouts  1.87 us (2%)
    pallas_call x1, Pallas kernels, per_device(): pl.pallas_call(kernel, out_shape=jax.ShapeDtypeStruct((1, ROWS, 1024), BF...  72.1 us
    unnamed x1, local copies, waits for them, and re-layouts  1.87 us

profile of v6, /device:TPU:1, one launch (start us, length us, event | category | flops | bytes accessed | tf_op | source)
XLA Modules:
  0.0 74.0 jit_solution(11071998894167517398)
XLA Ops:
  0.0 72.1 %shard_map.109 = bf16[1,256,1024]{2,1,0:T(8,128)(2,1)} custom-call(bf16[256,7680]{1,0:T(8,128)(2,1)} %bitcast.7, f32[10,128]{1,0:T(8,128)} %bitcast.10, bf16[480,1024]{1,0:T(8,128)(2,1)} %proj_hbm.1, bf16[1024,2048]{1,0:T(8,128)(2,1)} %kv_hbm.1, f32[1,128]{1,0:T(1,128)} %bitcast.11, bf16[16,16,1024]{2,1,0:T(8,128)(2,1)} %bitcast.8, f32[1,128]{1,0:T(1,128)} %bitcast.12, ...), custom_call_target="tpu_custom_call" | custom-call | tf_op jit(solution)/shard_map/pallas_call | solution.py:588
  72.1 1.9 %copy.13 = bf16[1,256,1024]{2,1,0:T(8,128)(2,1)} copy(bf16[1,256,1024]{2,1,0:T(8,128)(2,1)} %shard_map.109) | data formatting | bytes 1048576
